TPU v7x, 32 devices: a whole 2x2x4 slice. The times are simulated.
32 devices in a mesh: gx: 4 (over y, x), gy: 2 (over core), gz: 4 (over z).
Axes of the slice: x: 2, y: 2, z: 4, core: 2. Of those that a mesh axis runs over, the one named last changes fastest.
Arguments:
- fine: float32 [5, 64, 32, 512], P(None, 'gx', 'gy', 'gz'), as said below
- shell: float32 [4, 64, 3840], P('gx', ('gy', 'gz')), as said below
- parent: int32 [4, 64], P('gx'), may hold values from 0 to 63, as said below
- link: int32 [6, 4, 2, 32], P(None, 'gx', 'gy', 'gz'), may hold values 0 or 1
Outputs:
- fine_new: float32 [5, 64, 32, 512], P(None, 'gx', 'gy', 'gz')
- coarse_new: float32 [4, 64, 2560], P('gx', ('gy', 'gz'))
Inputs may be any that keep to these rules, and one draw needn't show every extreme that they name: Each row parent[i, :] names every slot 0 to 63 exactly once. Of the 8 blocks q = d * 8 to d * 8 + 7 of a row, at most 2 have parents among the slots o * 8 to o * 8 + 7 of any one o, and every such pair that meets at all holds exactly 2. `fine`: density and energy make pressure positive in every cell; velocities stay well below the sound speed times a few. `shell`: same physical ranges as fine.
All inputs are finite; a program needn't handle non-finite values. No bound on the sum of `link` on one device may be relied on, other than what follows from the above.
Results may differ from a plain program's by a relative error of at most 0.0003.
Values sent between devices are 32-bit elements; how exact they have to be, the bound alone decides.
A program may use at most 128 MiB of HBM per device.

v0:
```python
import functools

import jax
import jax.numpy as jnp
from jax import lax
from jax.experimental import pallas as pl
from jax.experimental.pallas import tpu as pltpu
from jax.sharding import PartitionSpec as P

BS = 16
GAMMA = 1.4
LAMBDA = 0.05
LANES = 128
MESH = pl.DeviceIdType.MESH
F32 = jnp.float32
BF16 = jnp.bfloat16


def iota(shape, dim):
    return lax.broadcasted_iota(jnp.int32, shape, dim)


def parts_of(x, count):
    result = []
    for _ in range(count - 1):
        head = x.astype(BF16).astype(F32)
        result.append(head)
        x = x - head
    result.append(x)
    return result


def dot(a, b, contract):
    return lax.dot_general(a, b, (contract, ((), ())), preferred_element_type=F32)


def stacked(x):
    pieces = parts_of(x, 3)
    if x.shape[0] % 16:
        pieces.append(jnp.zeros_like(x))
    return jnp.concatenate(pieces, axis=0).astype(BF16)


def beside(x, rows):
    count = 4 if rows % 16 else 3
    return jnp.concatenate([x] * count, axis=1).astype(BF16)


def prim(u):
    inv = 1.0 / u[0]
    vel = [u[1] * inv, u[2] * inv, u[3] * inv]
    press = (GAMMA - 1.0) * (u[4] - 0.5 * (u[1] * vel[0] + u[2] * vel[1] + u[3] * vel[2]))
    sound = jnp.sqrt(GAMMA * press * inv)
    return vel, press, sound


def flux(u, pr, d):
    vel, press, sound = pr
    vd = vel[d]
    f = [u[1 + d], u[1] * vd, u[2] * vd, u[3] * vd, (u[4] + press) * vd]
    f[1 + d] = f[1 + d] + press
    return f, jnp.abs(vd) + sound


def interface(ul, fl, sl, ur, fr, sr, sign=0.5):
    wave = sign * jnp.maximum(sl, sr)
    return [0.5 * (fl[i] + fr[i]) - wave * (ur[i] - ul[i]) for i in range(5)]


def kernel(
    n,
    fine, shell, parent, link, out, coarse,
    s0, s1, ypack, zpack, hx, hy, hz, sstage, srecv, rstage, rrecv, xt, cxy, cz, hyf, xy, zt,
    load_sem, halo_send, halo_recv, all_send, all_recv,
):
    nx, ny, nz = n
    group = ny * nz
    count = 2 * group
    gx, gy, gz = lax.axis_index("gx"), lax.axis_index("gy"), lax.axis_index("gz")
    me = gy * nz + gz
    blk = shell.shape[1]
    width = shell.shape[2] // 2
    chunks = width // LANES
    rwidth = coarse.shape[2]
    rchunks = rwidth // LANES
    nq = parent.shape[1]
    peers = []
    for i in range(1, group):
        peer = lax.rem(me + i, group)
        peers.append((gx, peer // nz, lax.rem(peer, nz)))
    xlo, xhi = (lax.rem(gx + nx - 1, nx), gy, gz), (lax.rem(gx + 1, nx), gy, gz)
    ylo, yhi = (gx, lax.rem(gy + ny - 1, ny), gz), (gx, lax.rem(gy + 1, ny), gz)
    zlo, zhi = (gx, gy, lax.rem(gz + nz - 1, nz)), (gx, gy, lax.rem(gz + 1, nz))

    barrier = pltpu.get_barrier_semaphore()
    greeted = peers + [xlo, xhi]
    for dev in greeted:
        pl.semaphore_signal(barrier, inc=1, device_id=dev, device_id_type=MESH)

    loads = []
    for f in range(5):
        load = pltpu.make_async_copy(fine.at[f], s0.at[f, pl.ds(BS, BS * BS)], load_sem.at[f])
        load.start()
        loads.append(load)

    par = parent[...]
    lane_q = iota((1, nq), 1)
    owner = par // blk
    rank = jnp.zeros((1, nq), jnp.int32)
    for j in range(1, blk):
        before = pltpu.roll(jnp.broadcast_to(owner, (8, nq)), j, 1)[0:1]
        rank = rank + jnp.where((lane_q % blk >= j) & (before == owner), 1, 0)
    at_owner = (lane_q // blk) * 2 + rank
    at_block = owner * 2 + rank
    to_t = (jnp.broadcast_to(at_owner, (count, nq)) == iota((count, nq), 0)).astype(F32).astype(BF16)
    mine = (jnp.broadcast_to(par, (blk, nq)) == me * blk + iota((blk, nq), 0)).astype(F32).astype(BF16)
    sel_ts = dot(to_t, mine, ((1,), (1,)))
    sel_st = dot(mine, to_t, ((1,), (1,)))
    at_block8 = jnp.broadcast_to(at_block.astype(F32), (8, nq)).astype(BF16)
    spread = (iota((nq, LANES), 0) == me * blk + iota((nq, LANES), 1) // BS).astype(F32).astype(BF16)
    pick = (iota((nq, blk), 0) == me * blk + iota((nq, blk), 1)).astype(F32).astype(BF16)
    row_lane = dot(at_block8, spread, ((1,), (0,)))[0:1]
    row_blk = dot(at_block8, pick, ((1,), (0,)))[0:1]
    be = (jnp.broadcast_to(row_lane, (count, LANES)) == iota((count, LANES), 0).astype(F32)).astype(F32)
    be3 = jnp.concatenate([be] * 3, axis=0).astype(BF16)
    sel_tk = (jnp.broadcast_to(row_blk, (count, blk)) == iota((count, blk), 0).astype(F32)).astype(F32)

    sel = beside(sel_ts, blk)
    for c in range(chunks):
        now = shell[0, :, pl.ds(c * LANES, LANES)]
        end = shell[0, :, pl.ds(width + c * LANES, LANES)]
        both = jnp.concatenate([stacked(now), stacked(0.5 * (now + end))], axis=1)
        rows = dot(sel, both, ((1,), (0,)))
        sstage[0, pl.ds(c, count, stride=16), :] = rows[:, :LANES]
        sstage[1, pl.ds(c, count, stride=16), :] = rows[:, LANES:]

    lane = iota((BS, LANES), 1)
    sub = iota((BS, LANES), 0)

    def plane(ref, f, x):
        return ref[f, pl.ds(pl.multiple_of((x + 1) * BS, BS), BS), :]

    def pack_y(ref):
        for f in range(5):
            ypack[0, f] = ref[f, pl.ds(BS, BS, stride=BS), :]
            ypack[1, f] = ref[f, pl.ds(2 * BS - 1, BS, stride=BS), :]

    def pack_z(ref):
        def body(x, acc):
            a0, a1 = acc
            for f in range(4):
                i = f * BS + x
                a0 = jnp.where(lane // 2 == i, pltpu.roll(plane(ref, f, x), 2 * i + 1, 1), a0)
            a1 = jnp.where(lane // 2 == x, pltpu.roll(plane(ref, 4, x), 2 * x + 1, 1), a1)
            return a0, a1

        zero = jnp.zeros((BS, LANES), F32)
        a0, a1 = lax.fori_loop(0, BS, body, (zero, zero))
        zpack[0] = a0
        zpack[1] = a1

    def halos(ref, step):
        def send(k, src, dst, dev):
            copy = pltpu.make_async_remote_copy(
                src_ref=src, dst_ref=dst, send_sem=halo_send.at[step, k], recv_sem=halo_recv.at[step, k],
                device_id=dev, device_id_type=MESH,
            )
            copy.start()
            return copy

        return [
            send(0, ref.at[:, pl.ds(BS * BS, BS)], hx.at[step, 0], xhi),
            send(1, ref.at[:, pl.ds(BS, BS)], hx.at[step, 1], xlo),
            send(2, ypack.at[1], hy.at[step, 0], yhi),
            send(3, ypack.at[0], hy.at[step, 1], ylo),
            send(4, zpack, hz.at[step, 0], zhi),
            send(5, zpack, hz.at[step, 1], zlo),
        ]

    def exchange(kind, stage, recv, rows):
        copies = []
        for i, dev in enumerate(peers):
            to = lax.rem(me + i + 1, group)
            copy = pltpu.make_async_remote_copy(
                src_ref=stage.at[pl.ds(pl.multiple_of(to * rows, 8), rows)],
                dst_ref=recv.at[pl.ds(pl.multiple_of(me * rows, 8), rows)],
                send_sem=all_send.at[kind, i], recv_sem=all_recv.at[kind, i],
                device_id=dev, device_id_type=MESH,
            )
            copy.start()
            copies.append(copy)
        own = pl.ds(pl.multiple_of(me * rows, 8), rows)
        recv[own, :] = stage[own, :]
        return copies

    for load in loads:
        load.wait()
    pl.semaphore_wait(barrier, len(greeted))
    now_copies = exchange(0, sstage.at[0], srecv.at[0], 32)
    pack_y(s0)
    pack_z(s0)
    halo0 = halos(s0, 0)
    mid_copies = exchange(1, sstage.at[1], srecv.at[1], 32)

    linkf = jnp.concatenate([link[k, 0] for k in range(6)] + [jnp.zeros((2, blk), jnp.int32)], axis=0)
    over = (iota((blk, LANES), 0) == iota((blk, LANES), 1) // BS).astype(F32).astype(BF16)
    mask = dot(linkf.astype(F32).astype(BF16), over, ((1,), (0,)))
    in_blk = lane % BS
    is_lo, is_hi = in_blk == 0, in_blk == BS - 1
    zmask = jnp.where(is_lo, mask[4:5], mask[5:6]) > 0.5
    sign = jnp.where(is_lo, 0.5, -0.5)
    ends = (lane == 0) | (lane == LANES - 1)
    half_lane = (iota((8, LANES), 1) % BS) // 2
    lo8 = iota((8, LANES), 1) % BS == 0

    def expand(level):
        for c in range(chunks):
            rows = srecv[level, pl.ds(c, count, stride=16), :]
            xt[pl.ds(c * LANES, LANES), :] = dot(stacked(rows), be3, ((0,), (0,)))
        for k in range(20):
            tile = xt[pl.ds(k * 64, 8, stride=8), :]
            for b in range(1, 8):
                tile = jnp.where(half_lane == b, xt[pl.ds(k * 64 + b, 8, stride=8), :], tile)
            cxy[pl.ds(k * BS, 8, stride=2), :] = tile
            cxy[pl.ds(k * BS + 1, 8, stride=2), :] = tile
        for k in range(40):
            tile = jnp.where(lo8, xt[pl.ds(1280 + k * 8, 8), :], xt[pl.ds(1600 + k * 8, 8), :])
            cz[pl.ds(k * BS, 8, stride=2), :] = tile
            cz[pl.ds(k * BS + 1, 8, stride=2), :] = tile

    def advance(ref, step, store):
        for side in range(2):
            chosen = jnp.broadcast_to(mask[side:side + 1], (BS, LANES)) > 0.5
            for f in range(5):
                ref[f, pl.ds(side * 17 * BS, BS), :] = jnp.where(
                    chosen, hx[step, side, f], cxy[pl.ds((side * 5 + f) * BS, BS), :]
                )
        for side in range(2):
            chosen = jnp.broadcast_to(mask[2 + side:3 + side], (BS, LANES)) > 0.5
            ghost = [
                jnp.where(chosen, hy[step, side, f], cxy[pl.ds(((2 + side) * 5 + f) * BS, BS), :])
                for f in range(5)
            ]
            cells = [ref[f, pl.ds(BS + side * (BS - 1), BS, stride=BS), :] for f in range(5)]
            gf, gs = flux(ghost, prim(ghost), 1)
            cf, cs = flux(cells, prim(cells), 1)
            face = interface(ghost, gf, gs, cells, cf, cs, 0.5 if side == 0 else -0.5)
            for f in range(5):
                hyf[pl.ds((side * 5 + f) * BS, BS), :] = face[f]
        comb = []
        for k in range(2):
            left = pltpu.roll(hz[step, 0, k], 1, 1)
            right = pltpu.roll(hz[step, 1, k], LANES - 1, 1)
            comb.append(jnp.where(lane % 2 == 0, right, left))

        ul = [plane(ref, f, -1) for f in range(5)]
        u = [plane(ref, f, 0) for f in range(5)]
        fl, sl = flux(ul, prim(ul), 0)
        pr = prim(u)
        fc, sc = flux(u, pr, 0)
        first = interface(ul, fl, sl, u, fc, sc)

        def body(x, carry):
            hxl, u, pr = carry
            un = [plane(ref, f, x + 1) for f in range(5)]
            prn = prim(un)
            fc, sc = flux(u, pr, 0)
            fn, sn = flux(un, prn, 0)
            hxr = interface(u, fc, sc, un, fn, sn)
            total = [hxr[f] - hxl[f] for f in range(5)]

            fc, sc = flux(u, pr, 1)
            ub = [pltpu.roll(a, 1, 0) for a in u]
            fb = [pltpu.roll(a, 1, 0) for a in fc]
            low = interface(ub, fb, pltpu.roll(sc, 1, 0), u, fc, sc)
            for f in range(5):
                lo = jnp.where(sub == 0, hyf[pl.ds(f * BS + x, 1), :], low[f])
                hi = jnp.where(sub == BS - 1, hyf[pl.ds((5 + f) * BS + x, 1), :], pltpu.roll(low[f], BS - 1, 0))
                total[f] = total[f] + (hi - lo)

            fc, sc = flux(u, pr, 2)
            ub = [pltpu.roll(a, 1, 1) for a in u]
            fb = [pltpu.roll(a, 1, 1) for a in fc]
            low = interface(ub, fb, pltpu.roll(sc, 1, 1), u, fc, sc)
            ghost = []
            for f in range(5):
                i = (f % 4) * BS + x
                far = pltpu.roll(comb[f // 4], LANES - 1 - 2 * i, 1)
                near = jnp.where(is_lo, ub[f], pltpu.roll(u[f], LANES - 1, 1))
                near = jnp.where(ends, far, near)
                at = pl.multiple_of((f * 8 + x // 2) * BS, BS)
                ghost.append(jnp.where(zmask, near, cz[pl.ds(at, BS), :]))
            ghost = [jnp.where(is_lo | is_hi, ghost[f], u[f]) for f in range(5)]
            gf, gs = flux(ghost, prim(ghost), 2)
            edge = interface(ghost, gf, gs, u, fc, sc, sign)
            for f in range(5):
                lo = jnp.where(is_lo, edge[f], low[f])
                hi = jnp.where(is_hi, edge[f], pltpu.roll(low[f], LANES - 1, 1))
                total[f] = total[f] + (hi - lo)
                store(f, x, u[f] - LAMBDA * total[f])
            return hxr, un, prn

        lax.fori_loop(0, BS, body, (first, u, pr))

    def store_mid(f, x, value):
        s1[f, pl.ds(pl.multiple_of((x + 1) * BS, BS), BS), :] = value

    def store_out(f, x, value):
        out[f, pl.ds(pl.multiple_of(x * BS, BS), BS), :] = value

    for copy in now_copies:
        copy.wait_recv()
    expand(0)
    for copy in halo0:
        copy.wait()
    advance(s0, 0, store_mid)
    pack_y(s1)
    pack_z(s1)
    halo1 = halos(s1, 1)
    for copy in mid_copies:
        copy.wait_recv()
    expand(1)
    for copy in halo1:
        copy.wait()
    advance(s1, 1, store_out)

    for f in range(5):
        for a in range(8):
            total = None
            for x in range(2):
                for y in range(2):
                    piece = out[f, pl.ds((2 * a + x) * BS + y, 8, stride=2), :]
                    total = piece if total is None else total + piece
            xy[pl.ds((f * 8 + a) * 8, 8), :] = 0.125 * total
    used = 5 * 64
    interleave = (iota((LANES, 8 * LANES), 0) == iota((LANES, 8 * LANES), 1) // 8).astype(F32).astype(BF16)
    lane8 = iota((blk, LANES), 1) % 8
    sel = beside(sel_tk, blk)
    for c in range((used + LANES - 1) // LANES):
        size = min(LANES, used - c * LANES)
        block = xy[pl.ds(c * LANES, LANES), :]
        if size < LANES:
            block = jnp.where(iota((LANES, LANES), 0) < size, block, 0.0)
        zt[...] = block.T
        rows = jnp.concatenate(
            [zt[pl.ds(2 * z, blk, stride=BS), :] + zt[pl.ds(2 * z + 1, blk, stride=BS), :] for z in range(8)],
            axis=0,
        )
        wide = dot(jnp.concatenate(parts_of(rows, 3), axis=0).astype(BF16), interleave, ((1,), (0,)))
        wide = wide[:64] + wide[64:128] + wide[128:]
        for g in range(size // 16):
            tile = wide[0:8, g * LANES:(g + 1) * LANES]
            for z in range(1, 8):
                tile = jnp.where(lane8 == z, wide[z * 8:z * 8 + 8, g * LANES:(g + 1) * LANES], tile)
            rstage[pl.ds(c * 8 + g, count, stride=rchunks), :] = dot(sel, stacked(tile), ((1,), (0,)))
    back = exchange(2, rstage, rrecv, 2 * rchunks)
    for copy in back:
        copy.wait_recv()
    sel = beside(sel_st, count)
    for c in range(rchunks):
        rows = rrecv[pl.ds(c, count, stride=rchunks), :]
        coarse[0, :, pl.ds(c * LANES, LANES)] = dot(sel, stacked(rows), ((1,), (0,)))
    for copy in now_copies + mid_copies + back:
        copy.wait_send()


def shards(n, fine, shell, parent, link):
    group = n[1] * n[2]
    count = 2 * group
    rwidth = 5 * (BS // 2) ** 3
    fine2 = fine.reshape(5, BS * BS, LANES)
    vmem = pl.BlockSpec(memory_space=pltpu.VMEM)
    out, coarse = pl.pallas_call(
        functools.partial(kernel, n),
        out_shape=(
            jax.ShapeDtypeStruct((5, BS * BS, LANES), F32),
            jax.ShapeDtypeStruct((1, shell.shape[1], rwidth), F32),
        ),
        in_specs=[pl.BlockSpec(memory_space=pl.ANY), vmem, vmem, vmem],
        out_specs=(vmem, vmem),
        scratch_shapes=[
            pltpu.VMEM((5, 18 * BS, LANES), F32),
            pltpu.VMEM((5, 18 * BS, LANES), F32),
            pltpu.VMEM((2, 5, BS, LANES), F32),
            pltpu.VMEM((2, BS, LANES), F32),
            pltpu.VMEM((2, 2, 5, BS, LANES), F32),
            pltpu.VMEM((2, 2, 5, BS, LANES), F32),
            pltpu.VMEM((2, 2, 2, BS, LANES), F32),
            pltpu.VMEM((2, count * 16, LANES), F32),
            pltpu.VMEM((2, count * 16, LANES), F32),
            pltpu.VMEM((count * (rwidth // LANES), LANES), F32),
            pltpu.VMEM((count * (rwidth // LANES), LANES), F32),
            pltpu.VMEM((1920, LANES), F32),
            pltpu.VMEM((20 * BS, LANES), F32),
            pltpu.VMEM((40 * BS, LANES), F32),
            pltpu.VMEM((10 * BS, LANES), F32),
            pltpu.VMEM((384, LANES), F32),
            pltpu.VMEM((LANES, LANES), F32),
            pltpu.SemaphoreType.DMA((5,)),
            pltpu.SemaphoreType.DMA((2, 6)),
            pltpu.SemaphoreType.DMA((2, 6)),
            pltpu.SemaphoreType.DMA((3, group)),
            pltpu.SemaphoreType.DMA((3, group)),
        ],
        compiler_params=pltpu.CompilerParams(
            collective_id=0, has_side_effects=True, vmem_limit_bytes=32 * 1024 * 1024
        ),
    )(fine2, shell, parent, link)
    return out.reshape(fine.shape), coarse


def solution(mesh):
    n = (mesh.shape["gx"], mesh.shape["gy"], mesh.shape["gz"])
    return jax.shard_map(
        functools.partial(shards, n),
        mesh=mesh,
        in_specs=(
            P(None, "gx", "gy", "gz"),
            P("gx", ("gy", "gz"), None),
            P("gx", None),
            P(None, "gx", "gy", "gz"),
        ),
        out_specs=(P(None, "gx", "gy", "gz"), P("gx", ("gy", "gz"), None)),
        check_vma=False,
    )
```

profile of v0, /device:TPU:0, one launch (start us, length us, event | category | flops | bytes accessed | tf_op | source)
XLA Modules:
  0.0 34.3 jit_solution(11487843022011177380)
XLA Ops:
  0.6 0.0 copy-start.3
  0.6 0.6 %copy-done.3 = s32[1,64]{1,0:T(1,128)S(1)} copy-done((s32[1,64]{1,0:T(1,128)S(1)}, s32[1,64]{1,0:T(1,128)}, u32[]{:S(2)}) %copy-start.3) | copy-done | bytes 280
  1.3 0.0 copy-start
  1.3 1.1 %copy-done = f32[5,16,16,128]{3,2,1,0:T(8,128)S(1)} copy-done((f32[5,16,16,128]{3,2,1,0:T(8,128)S(1)}, f32[5,16,16,128]{3,2,1,0:T(8,128)}, u32[]{:S(2)}) %copy-start) | copy-done | bytes 655384
  2.4 0.0 copy-start.1
  2.4 0.9 %copy-done.1 = f32[1,8,3840]{2,1,0:T(8,128)S(1)} copy-done((f32[1,8,3840]{2,1,0:T(8,128)S(1)}, f32[1,8,3840]{2,1,0:T(8,128)}, u32[]{:S(2)}) %copy-start.1) | copy-done | bytes 122904
  3.3 0.0 copy-start.2
  3.3 0.7 %copy-done.2 = s32[6,1,1,8]{3,2,1,0:T(1,128)S(1)} copy-done((s32[6,1,1,8]{3,2,1,0:T(1,128)S(1)}, s32[6,1,1,8]{3,2,1,0:T(1,128)}, u32[]{:S(2)}) %copy-start.2) | copy-done | bytes 216
  4.0 28.9 %shard_map.59 = (f32[5,256,128]{2,1,0:T(8,128)S(1)}, f32[1,8,2560]{2,1,0:T(8,128)S(1)}) custom-call(f32[5,256,128]{2,1,0:T(8,128)S(1)} %bitcast.2, f32[1,8,3840]{2,1,0:T(8,128)S(1)} %copy-done.1, s32[1,64]{1,0:T(1,128)S(1)} %copy-done.3, s32[6,1,1,8]{3,2,1,0:T(1,128)S(1)} %copy-done.2), custom_call_target="tpu_custom_call" | custom-call | tf_op jit(solution)/shard_map/pallas_call | solution.py:373
  32.8 0.8 %copy.8 = f32[5,16,16,128]{3,2,1,0:T(8,128)} copy(f32[5,16,16,128]{3,2,1,0:T(8,128)S(1)} %bitcast.3) | data formatting | bytes 1310720
  33.7 0.6 %copy.9 = f32[1,8,2560]{2,1,0:T(8,128)} copy(f32[1,8,2560]{2,1,0:T(8,128)S(1)} %get-tuple-element.9) | data formatting | bytes 163840
Async XLA Ops:
  0.6 0.7 %copy-start.3 = (s32[1,64]{1,0:T(1,128)S(1)}, s32[1,64]{1,0:T(1,128)}, u32[]{:S(2)}) copy-start(s32[1,64]{1,0:T(1,128)} %parent.1) | copy-start | bytes 772
  1.3 1.1 %copy-start = (f32[5,16,16,128]{3,2,1,0:T(8,128)S(1)}, f32[5,16,16,128]{3,2,1,0:T(8,128)}, u32[]{:S(2)}) copy-start(f32[5,16,16,128]{3,2,1,0:T(8,128)} %param.4) | copy-start | bytes 1966084
  2.4 0.9 %copy-start.1 = (f32[1,8,3840]{2,1,0:T(8,128)S(1)}, f32[1,8,3840]{2,1,0:T(8,128)}, u32[]{:S(2)}) copy-start(f32[1,8,3840]{2,1,0:T(8,128)} %shell.1) | copy-start | bytes 368644
  3.3 0.7 %copy-start.2 = (s32[6,1,1,8]{3,2,1,0:T(1,128)S(1)}, s32[6,1,1,8]{3,2,1,0:T(1,128)}, u32[]{:S(2)}) copy-start(s32[6,1,1,8]{3,2,1,0:T(1,128)} %link.1) | copy-start | bytes 580
where the time goes:
time: 34.5 us; the launch traced here: 34.3 us
  Pallas kernels  28.9 us (84%)
  local copies, waits for them, and re-layouts  4.79 us (14%)
  between operations  0.65 us (2%)
    pallas_call x1, Pallas kernels, shards(): pl.pallas_call(functools.partial(kernel, n), out_shape=(jax.ShapeDtypeStr...  28.9 us
    unnamed x10, local copies, waits for them, and re-layouts  4.79 us

commit v1 on v0

--- a/solution.py
+++ b/solution.py
@@ -69,8 +69,8 @@
 
 def kernel(
     n,
-    fine, shell, parent, link, out, coarse,
-    s0, s1, ypack, zpack, hx, hy, hz, sstage, srecv, rstage, rrecv, xt, cxy, cz, hyf, xy, zt,
+    fine, shell_hbm, parent_hbm, link_hbm, out_hbm, coarse,
+    out, shell, parent, link, s0, s1, ypack, zpack, hx, hy, hz, sstage, srecv, rstage, rrecv, xt, cxy, cz, hyf, xy, zt,
     load_sem, halo_send, halo_recv, all_send, all_recv,
 ):
     nx, ny, nz = n
@@ -98,11 +98,16 @@
         pl.semaphore_signal(barrier, inc=1, device_id=dev, device_id_type=MESH)
 
     loads = []
+    for k, (src, dst) in enumerate(((parent_hbm, parent), (shell_hbm, shell), (link_hbm, link))):
+        load = pltpu.make_async_copy(src, dst, load_sem.at[5 + k])
+        load.start()
+        loads.append(load)
     for f in range(5):
         load = pltpu.make_async_copy(fine.at[f], s0.at[f, pl.ds(BS, BS * BS)], load_sem.at[f])
         load.start()
         loads.append(load)
 
+    loads[0].wait()
     par = parent[...]
     lane_q = iota((1, nq), 1)
     owner = par // blk
@@ -125,6 +130,7 @@
     be3 = jnp.concatenate([be] * 3, axis=0).astype(BF16)
     sel_tk = (jnp.broadcast_to(row_blk, (count, blk)) == iota((count, blk), 0).astype(F32)).astype(F32)
 
+    loads[1].wait()
     sel = beside(sel_ts, blk)
     for c in range(chunks):
         now = shell[0, :, pl.ds(c * LANES, LANES)]
@@ -155,7 +161,7 @@
             return a0, a1
 
         zero = jnp.zeros((BS, LANES), F32)
-        a0, a1 = lax.fori_loop(0, BS, body, (zero, zero))
+        a0, a1 = lax.fori_loop(0, BS, body, (zero, zero), unroll=True)
         zpack[0] = a0
         zpack[1] = a1
 
@@ -193,7 +199,7 @@
         recv[own, :] = stage[own, :]
         return copies
 
-    for load in loads:
+    for load in loads[2:]:
         load.wait()
     pl.semaphore_wait(barrier, len(greeted))
     now_copies = exchange(0, sstage.at[0], srecv.at[0], 32)
@@ -300,7 +306,7 @@
                 store(f, x, u[f] - LAMBDA * total[f])
             return hxr, un, prn
 
-        lax.fori_loop(0, BS, body, (first, u, pr))
+        lax.fori_loop(0, BS, body, (first, u, pr), unroll=2)
 
     def store_mid(f, x, value):
         s1[f, pl.ds(pl.multiple_of((x + 1) * BS, BS), BS), :] = value
@@ -323,6 +329,8 @@
     for copy in halo1:
         copy.wait()
     advance(s1, 1, store_out)
+    result = pltpu.make_async_copy(out, out_hbm, load_sem.at[8])
+    result.start()
 
     for f in range(5):
         for a in range(8):
@@ -362,6 +370,7 @@
         coarse[0, :, pl.ds(c * LANES, LANES)] = dot(sel, stacked(rows), ((1,), (0,)))
     for copy in now_copies + mid_copies + back:
         copy.wait_send()
+    result.wait()
 
 
 def shards(n, fine, shell, parent, link):
@@ -376,9 +385,13 @@
             jax.ShapeDtypeStruct((5, BS * BS, LANES), F32),
             jax.ShapeDtypeStruct((1, shell.shape[1], rwidth), F32),
         ),
-        in_specs=[pl.BlockSpec(memory_space=pl.ANY), vmem, vmem, vmem],
-        out_specs=(vmem, vmem),
+        in_specs=[pl.BlockSpec(memory_space=pltpu.HBM)] * 4,
+        out_specs=(pl.BlockSpec(memory_space=pltpu.HBM), vmem),
         scratch_shapes=[
+            pltpu.VMEM((5, BS * BS, LANES), F32),
+            pltpu.VMEM(shell.shape, F32),
+            pltpu.VMEM(parent.shape, jnp.int32),
+            pltpu.VMEM(link.shape, jnp.int32),
             pltpu.VMEM((5, 18 * BS, LANES), F32),
             pltpu.VMEM((5, 18 * BS, LANES), F32),
             pltpu.VMEM((2, 5, BS, LANES), F32),
@@ -396,14 +409,14 @@
             pltpu.VMEM((10 * BS, LANES), F32),
             pltpu.VMEM((384, LANES), F32),
             pltpu.VMEM((LANES, LANES), F32),
-            pltpu.SemaphoreType.DMA((5,)),
+            pltpu.SemaphoreType.DMA((9,)),
             pltpu.SemaphoreType.DMA((2, 6)),
             pltpu.SemaphoreType.DMA((2, 6)),
             pltpu.SemaphoreType.DMA((3, group)),
             pltpu.SemaphoreType.DMA((3, group)),
         ],
         compiler_params=pltpu.CompilerParams(
-            collective_id=0, has_side_effects=True, vmem_limit_bytes=32 * 1024 * 1024
+            collective_id=0, has_side_effects=True, vmem_limit_bytes=62 * 1024 * 1024
         ),
     )(fine2, shell, parent, link)
     return out.reshape(fine.shape), coarse

time: 34.5 us -> 30.5 us (0.88)
  local copies, waits for them, and re-layouts: 4.79 us -> 2.66 us
  Pallas kernels: 28.9 us -> 27 us
    unnamed x10 -> x4, local copies, waits for them, and re-layouts: 4.79 us -> 2.66 us
    pallas_call x1, Pallas kernels: 28.9 us -> 27 us  [shards(): pl.pallas_call(functools.partial(kernel, n), out_shape=(jax.ShapeDtypeStr...]
where the time goes in v1:
time: 30.5 us; the launch traced here: 30.3 us
  Pallas kernels  27 us (89%)
  local copies, waits for them, and re-layouts  2.66 us (9%)
  between operations  0.65 us (2%)
    pallas_call x1, Pallas kernels, shards(): pl.pallas_call(functools.partial(kernel, n), out_shape=(jax.ShapeDtypeStr...  27 us
    unnamed x4, local copies, waits for them, and re-layouts  2.66 us

profile of v1, /device:TPU:0, one launch (start us, length us, event | category | flops | bytes accessed | tf_op | source)
XLA Modules:
  0.0 30.3 jit_solution(12983479684307415609)
XLA Ops:
  0.6 27.0 %shard_map.59 = (f32[5,256,128]{2,1,0:T(8,128)}, f32[1,8,2560]{2,1,0:T(8,128)}) custom-call(f32[5,256,128]{2,1,0:T(8,128)} %bitcast.2, f32[1,8,3840]{2,1,0:T(8,128)} %shell_hbm.1, s32[1,64]{1,0:T(1,128)} %parent_hbm.1, s32[6,1,1,8]{3,2,1,0:T(1,128)} %link_hbm.1), custom_call_target="tpu_custom_call" | custom-call | tf_op jit(solution)/shard_map/pallas_call | solution.py:382
  27.6 0.0 copy-start
  27.6 2.0 %copy.8 = f32[5,16,16,128]{3,2,1,0:T(8,128)} copy(f32[5,16,16,128]{3,2,1,0:T(8,128)} %bitcast.3) | data formatting | bytes 1310720
  29.7 0.0 copy-done
  29.7 0.6 %copy.9 = f32[1,8,2560]{2,1,0:T(8,128)} copy(f32[1,8,2560]{2,1,0:T(8,128)S(1)} %copy-done) | data formatting | bytes 163840
Async XLA Ops:
  27.6 2.0 %copy-start = (f32[1,8,2560]{2,1,0:T(8,128)S(1)}, f32[1,8,2560]{2,1,0:T(8,128)}, u32[]{:S(2)}) copy-start(f32[1,8,2560]{2,1,0:T(8,128)} %get-tuple-element.9) | copy-start | bytes 245764

commit v2 on v1

--- a/solution.py
+++ b/solution.py
@@ -70,7 +70,7 @@
 def kernel(
     n,
     fine, shell_hbm, parent_hbm, link_hbm, out_hbm, coarse,
-    out, shell, parent, link, s0, s1, ypack, zpack, hx, hy, hz, sstage, srecv, rstage, rrecv, xt, cxy, cz, hyf, xy, zt,
+    out, shell, parent, link, s0, s1, ypack, zpack, hx, hy, hz, sstage, srecv, rstage, rrecv, xt, cxy, cz, cells_z, xy, zt,
     load_sem, halo_send, halo_recv, all_send, all_recv,
 ):
     nx, ny, nz = n
@@ -103,7 +103,7 @@
         load.start()
         loads.append(load)
     for f in range(5):
-        load = pltpu.make_async_copy(fine.at[f], s0.at[f, pl.ds(BS, BS * BS)], load_sem.at[f])
+        load = pltpu.make_async_copy(fine.at[f], s0.at[f], load_sem.at[f])
         load.start()
         loads.append(load)
 
@@ -125,9 +125,14 @@
     spread = (iota((nq, LANES), 0) == me * blk + iota((nq, LANES), 1) // BS).astype(F32).astype(BF16)
     pick = (iota((nq, blk), 0) == me * blk + iota((nq, blk), 1)).astype(F32).astype(BF16)
     row_lane = dot(at_block8, spread, ((1,), (0,)))[0:1]
+    block_hi = ((iota((nq, LANES), 1) + 1) // BS + blk - 1) % blk
+    spread_hi = (iota((nq, LANES), 0) == me * blk + block_hi).astype(F32).astype(BF16)
+    row_lane_hi = dot(at_block8, spread_hi, ((1,), (0,)))[0:1]
     row_blk = dot(at_block8, pick, ((1,), (0,)))[0:1]
     be = (jnp.broadcast_to(row_lane, (count, LANES)) == iota((count, LANES), 0).astype(F32)).astype(F32)
     be3 = jnp.concatenate([be] * 3, axis=0).astype(BF16)
+    be_hi = (jnp.broadcast_to(row_lane_hi, (count, LANES)) == iota((count, LANES), 0).astype(F32)).astype(F32)
+    be3_hi = jnp.concatenate([be_hi] * 3, axis=0).astype(BF16)
     sel_tk = (jnp.broadcast_to(row_blk, (count, blk)) == iota((count, blk), 0).astype(F32)).astype(F32)
 
     loads[1].wait()
@@ -142,28 +147,31 @@
 
     lane = iota((BS, LANES), 1)
     sub = iota((BS, LANES), 0)
+    even = lane % 2 == 0
+    pair = ((lane + 1) // 2) % 8
+    first_pairs = (lane + 1) % LANES < 16
 
     def plane(ref, f, x):
-        return ref[f, pl.ds(pl.multiple_of((x + 1) * BS, BS), BS), :]
+        return ref[f, pl.ds(x * BS, BS), :]
 
     def pack_y(ref):
         for f in range(5):
-            ypack[0, f] = ref[f, pl.ds(BS, BS, stride=BS), :]
-            ypack[1, f] = ref[f, pl.ds(2 * BS - 1, BS, stride=BS), :]
+            ypack[0, f] = ref[f, pl.ds(0, BS, stride=BS), :]
+            ypack[1, f] = ref[f, pl.ds(BS - 1, BS, stride=BS), :]
 
     def pack_z(ref):
-        def body(x, acc):
-            a0, a1 = acc
-            for f in range(4):
-                i = f * BS + x
-                a0 = jnp.where(lane // 2 == i, pltpu.roll(plane(ref, f, x), 2 * i + 1, 1), a0)
-            a1 = jnp.where(lane // 2 == x, pltpu.roll(plane(ref, 4, x), 2 * x + 1, 1), a1)
-            return a0, a1
-
-        zero = jnp.zeros((BS, LANES), F32)
-        a0, a1 = lax.fori_loop(0, BS, body, (zero, zero), unroll=True)
-        zpack[0] = a0
-        zpack[1] = a1
+        packed = [jnp.zeros((BS, LANES), F32)] * 2
+        for f in range(5):
+            for g in range(2):
+                tile = plane(ref, f, 8 * g)
+                for x in range(1, 8):
+                    tile = jnp.where(pair == x, pltpu.roll(plane(ref, f, 8 * g + x), 2 * x, 1), tile)
+                k = f * 2 + g
+                cells_z[k] = tile
+                moved = tile if k % 8 == 0 else pltpu.roll(tile, 16 * (k % 8), 1)
+                packed[k // 8] = jnp.where(((lane + 1) // 16) % 8 == k % 8, moved, packed[k // 8])
+        zpack[0] = packed[0]
+        zpack[1] = packed[1]
 
     def halos(ref, step):
         def send(k, src, dst, dev):
@@ -175,8 +183,8 @@
             return copy
 
         return [
-            send(0, ref.at[:, pl.ds(BS * BS, BS)], hx.at[step, 0], xhi),
-            send(1, ref.at[:, pl.ds(BS, BS)], hx.at[step, 1], xlo),
+            send(0, ref.at[:, pl.ds(BS * BS - BS, BS)], hx.at[step, 0], xhi),
+            send(1, ref.at[:, pl.ds(0, BS)], hx.at[step, 1], xlo),
             send(2, ypack.at[1], hy.at[step, 0], yhi),
             send(3, ypack.at[0], hy.at[step, 1], ylo),
             send(4, zpack, hz.at[step, 0], zhi),
@@ -210,125 +218,139 @@
 
     linkf = jnp.concatenate([link[k, 0] for k in range(6)] + [jnp.zeros((2, blk), jnp.int32)], axis=0)
     over = (iota((blk, LANES), 0) == iota((blk, LANES), 1) // BS).astype(F32).astype(BF16)
-    mask = dot(linkf.astype(F32).astype(BF16), over, ((1,), (0,)))
-    in_blk = lane % BS
-    is_lo, is_hi = in_blk == 0, in_blk == BS - 1
-    zmask = jnp.where(is_lo, mask[4:5], mask[5:6]) > 0.5
-    sign = jnp.where(is_lo, 0.5, -0.5)
-    ends = (lane == 0) | (lane == LANES - 1)
+    over_hi = (iota((blk, LANES), 0) == ((iota((blk, LANES), 1) + 1) // BS + blk - 1) % blk).astype(F32).astype(BF16)
+    linkb = linkf.astype(F32).astype(BF16)
+    mask = dot(linkb, over, ((1,), (0,)))
+    mask_hi = dot(linkb, over_hi, ((1,), (0,)))
+    is_lo = lane % BS == 0
+    at_end = is_lo | (lane % BS == BS - 1)
+    zmask = jnp.where(even, mask[4:5], mask_hi[5:6]) > 0.5
     half_lane = (iota((8, LANES), 1) % BS) // 2
-    lo8 = iota((8, LANES), 1) % BS == 0
+    even8 = iota((8, LANES), 1) % 2 == 0
+    pair8 = (((iota((8, LANES), 1) + 1) // 2) % 8) // 2
 
     def expand(level):
         for c in range(chunks):
-            rows = srecv[level, pl.ds(c, count, stride=16), :]
-            xt[pl.ds(c * LANES, LANES), :] = dot(stacked(rows), be3, ((0,), (0,)))
+            rows = stacked(srecv[level, pl.ds(c, count, stride=16), :])
+            if c * LANES < 1600:
+                xt[pl.ds(c * LANES, LANES), :] = dot(rows, be3, ((0,), (0,)))
+            if (c + 1) * LANES > 1600:
+                skip = max(0, 1600 - c * LANES)
+                xt[pl.ds(c * LANES + skip, LANES - skip), :] = dot(rows, be3_hi, ((0,), (0,)))[skip:]
         for k in range(20):
             tile = xt[pl.ds(k * 64, 8, stride=8), :]
             for b in range(1, 8):
                 tile = jnp.where(half_lane == b, xt[pl.ds(k * 64 + b, 8, stride=8), :], tile)
             cxy[pl.ds(k * BS, 8, stride=2), :] = tile
             cxy[pl.ds(k * BS + 1, 8, stride=2), :] = tile
-        for k in range(40):
-            tile = jnp.where(lo8, xt[pl.ds(1280 + k * 8, 8), :], xt[pl.ds(1600 + k * 8, 8), :])
+        for k in range(10):
+            tile = None
+            for a in range(4):
+                at = ((k // 2) * 8 + 4 * (k % 2) + a) * 8
+                piece = jnp.where(even8, xt[pl.ds(1280 + at, 8), :], xt[pl.ds(1600 + at, 8), :])
+                tile = piece if a == 0 else jnp.where(pair8 == a, piece, tile)
             cz[pl.ds(k * BS, 8, stride=2), :] = tile
             cz[pl.ds(k * BS + 1, 8, stride=2), :] = tile
 
-    def advance(ref, step, store):
-        for side in range(2):
-            chosen = jnp.broadcast_to(mask[side:side + 1], (BS, LANES)) > 0.5
+    def inner(ref, dst):
+        def step_x(x, hxl, u, pr, last):
+            if last:
+                total = [-hxl[f] for f in range(5)]
+                hxr, un, prn = hxl, u, pr
+            else:
+                at = pl.multiple_of((x + 1) * BS, BS)
+                un = [ref[f, pl.ds(at, BS), :] for f in range(5)]
+                prn = prim(un)
+                fc, sc = flux(u, pr, 0)
+                fn, sn = flux(un, prn, 0)
+                hxr = interface(u, fc, sc, un, fn, sn)
+                total = [hxr[f] - hxl[f] for f in range(5)]
+            for d, axis, edge in ((1, 0, sub == 0), (2, 1, is_lo)):
+                fc, sc = flux(u, pr, d)
+                ub = [pltpu.roll(a, 1, axis) for a in u]
+                fb = [pltpu.roll(a, 1, axis) for a in fc]
+                low = interface(ub, fb, pltpu.roll(sc, 1, axis), u, fc, sc)
+                for f in range(5):
+                    lo = jnp.where(edge, 0.0, low[f])
+                    total[f] = total[f] + (pltpu.roll(lo, lo.shape[axis] - 1, axis) - lo)
+            at = pl.multiple_of(x * BS, BS)
             for f in range(5):
-                ref[f, pl.ds(side * 17 * BS, BS), :] = jnp.where(
-                    chosen, hx[step, side, f], cxy[pl.ds((side * 5 + f) * BS, BS), :]
-                )
-        for side in range(2):
-            chosen = jnp.broadcast_to(mask[2 + side:3 + side], (BS, LANES)) > 0.5
-            ghost = [
-                jnp.where(chosen, hy[step, side, f], cxy[pl.ds(((2 + side) * 5 + f) * BS, BS), :])
-                for f in range(5)
-            ]
-            cells = [ref[f, pl.ds(BS + side * (BS - 1), BS, stride=BS), :] for f in range(5)]
-            gf, gs = flux(ghost, prim(ghost), 1)
-            cf, cs = flux(cells, prim(cells), 1)
-            face = interface(ghost, gf, gs, cells, cf, cs, 0.5 if side == 0 else -0.5)
-            for f in range(5):
-                hyf[pl.ds((side * 5 + f) * BS, BS), :] = face[f]
+                dst[f, pl.ds(at, BS), :] = u[f] - LAMBDA * total[f]
+            return hxr, un, prn
+
+        u = [plane(ref, f, 0) for f in range(5)]
+        zero = [jnp.zeros((BS, LANES), F32)] * 5
+        carry = lax.fori_loop(
+            0, BS - 1, lambda x, carry: step_x(x, *carry, False), (zero, u, prim(u)), unroll=3
+        )
+        step_x(BS - 1, *carry, True)
+
+    def faces(ghost, cells, d, sign):
+        gf, gs = flux(ghost, prim(ghost), d)
+        cf, cs = flux(cells, prim(cells), d)
+        return interface(ghost, gf, gs, cells, cf, cs, sign)
+
+    def outer(ref, dst, step):
+        for d in range(2):
+            for side in range(2):
+                chosen = jnp.broadcast_to(mask[2 * d + side:2 * d + side + 1], (BS, LANES)) > 0.5
+                halo = hx if d == 0 else hy
+                if d == 0:
+                    rows = pl.ds(side * (BS - 1) * BS, BS)
+                else:
+                    rows = pl.ds(side * (BS - 1), BS, stride=BS)
+                ghost = [
+                    jnp.where(chosen, halo[step, side, f], cxy[pl.ds(((2 * d + side) * 5 + f) * BS, BS), :])
+                    for f in range(5)
+                ]
+                cells = [ref[f, rows, :] for f in range(5)]
+                face = faces(ghost, cells, d, 0.5 - side)
+                for f in range(5):
+                    dst[f, rows, :] = dst[f, rows, :] + (LAMBDA - 2 * side * LAMBDA) * face[f]
         comb = []
         for k in range(2):
             left = pltpu.roll(hz[step, 0, k], 1, 1)
             right = pltpu.roll(hz[step, 1, k], LANES - 1, 1)
-            comb.append(jnp.where(lane % 2 == 0, right, left))
-
-        ul = [plane(ref, f, -1) for f in range(5)]
-        u = [plane(ref, f, 0) for f in range(5)]
-        fl, sl = flux(ul, prim(ul), 0)
-        pr = prim(u)
-        fc, sc = flux(u, pr, 0)
-        first = interface(ul, fl, sl, u, fc, sc)
-
-        def body(x, carry):
-            hxl, u, pr = carry
-            un = [plane(ref, f, x + 1) for f in range(5)]
-            prn = prim(un)
-            fc, sc = flux(u, pr, 0)
-            fn, sn = flux(un, prn, 0)
-            hxr = interface(u, fc, sc, un, fn, sn)
-            total = [hxr[f] - hxl[f] for f in range(5)]
-
-            fc, sc = flux(u, pr, 1)
-            ub = [pltpu.roll(a, 1, 0) for a in u]
-            fb = [pltpu.roll(a, 1, 0) for a in fc]
-            low = interface(ub, fb, pltpu.roll(sc, 1, 0), u, fc, sc)
+            comb.append(jnp.where(even, left, right))
+        sign = jnp.where(even, 0.5, -0.5)
+        scale = jnp.where(even, LAMBDA, -LAMBDA)
+        for g in range(2):
+            cells, ghost = [], []
             for f in range(5):
-                lo = jnp.where(sub == 0, hyf[pl.ds(f * BS + x, 1), :], low[f])
-                hi = jnp.where(sub == BS - 1, hyf[pl.ds((5 + f) * BS + x, 1), :], pltpu.roll(low[f], BS - 1, 0))
-                total[f] = total[f] + (hi - lo)
-
-            fc, sc = flux(u, pr, 2)
-            ub = [pltpu.roll(a, 1, 1) for a in u]
-            fb = [pltpu.roll(a, 1, 1) for a in fc]
-            low = interface(ub, fb, pltpu.roll(sc, 1, 1), u, fc, sc)
-            ghost = []
+                k = f * 2 + g
+                tile = cells_z[k]
+                near = jnp.where(even, pltpu.roll(tile, 1, 1), pltpu.roll(tile, LANES - 1, 1))
+                far = comb[k // 8]
+                if k % 8:
+                    far = pltpu.roll(far, LANES - 16 * (k % 8), 1)
+                fine_side = jnp.where(first_pairs, far, near)
+                cells.append(tile)
+                ghost.append(jnp.where(zmask, fine_side, cz[pl.ds(k * BS, BS), :]))
+            face = faces(ghost, cells, 2, sign)
             for f in range(5):
-                i = (f % 4) * BS + x
-                far = pltpu.roll(comb[f // 4], LANES - 1 - 2 * i, 1)
-                near = jnp.where(is_lo, ub[f], pltpu.roll(u[f], LANES - 1, 1))
-                near = jnp.where(ends, far, near)
-                at = pl.multiple_of((f * 8 + x // 2) * BS, BS)
-                ghost.append(jnp.where(zmask, near, cz[pl.ds(at, BS), :]))
-            ghost = [jnp.where(is_lo | is_hi, ghost[f], u[f]) for f in range(5)]
-            gf, gs = flux(ghost, prim(ghost), 2)
-            edge = interface(ghost, gf, gs, u, fc, sc, sign)
-            for f in range(5):
-                lo = jnp.where(is_lo, edge[f], low[f])
-                hi = jnp.where(is_hi, edge[f], pltpu.roll(low[f], LANES - 1, 1))
-                total[f] = total[f] + (hi - lo)
-                store(f, x, u[f] - LAMBDA * total[f])
-            return hxr, un, prn
-
-        lax.fori_loop(0, BS, body, (first, u, pr), unroll=2)
-
-    def store_mid(f, x, value):
-        s1[f, pl.ds(pl.multiple_of((x + 1) * BS, BS), BS), :] = value
-
-    def store_out(f, x, value):
-        out[f, pl.ds(pl.multiple_of(x * BS, BS), BS), :] = value
-
+                change = scale * face[f]
+                for x in range(8):
+                    moved = change if x == 0 else pltpu.roll(change, LANES - 2 * x, 1)
+                    rows = pl.ds((8 * g + x) * BS, BS)
+                    dst[f, rows, :] = dst[f, rows, :] + jnp.where(at_end, moved, 0.0)
+
+    inner(s0, s1)
     for copy in now_copies:
         copy.wait_recv()
     expand(0)
     for copy in halo0:
         copy.wait()
-    advance(s0, 0, store_mid)
+    outer(s0, s1, 0)
     pack_y(s1)
     pack_z(s1)
     halo1 = halos(s1, 1)
     for copy in mid_copies:
         copy.wait_recv()
     expand(1)
+    inner(s1, out)
     for copy in halo1:
         copy.wait()
-    advance(s1, 1, store_out)
+    outer(s1, out, 1)
     result = pltpu.make_async_copy(out, out_hbm, load_sem.at[8])
     result.start()
 
@@ -373,6 +395,19 @@
     result.wait()
 
 
+def place(out, coarse, out_new, coarse_new, sem):
+    copies = [pltpu.make_async_copy(coarse, coarse_new, sem.at[10])]
+    half = out.shape[1] // 2
+    for f in range(5):
+        for k in range(2):
+            rows = pl.ds(k * half, half)
+            copies.append(pltpu.make_async_copy(out.at[f, rows], out_new.at[f, rows], sem.at[f * 2 + k]))
+    for copy in copies:
+        copy.start()
+    for copy in copies:
+        copy.wait()
+
+
 def shards(n, fine, shell, parent, link):
     group = n[1] * n[2]
     count = 2 * group
@@ -392,8 +427,8 @@
             pltpu.VMEM(shell.shape, F32),
             pltpu.VMEM(parent.shape, jnp.int32),
             pltpu.VMEM(link.shape, jnp.int32),
-            pltpu.VMEM((5, 18 * BS, LANES), F32),
-            pltpu.VMEM((5, 18 * BS, LANES), F32),
+            pltpu.VMEM((5, BS * BS, LANES), F32),
+            pltpu.VMEM((5, BS * BS, LANES), F32),
             pltpu.VMEM((2, 5, BS, LANES), F32),
             pltpu.VMEM((2, BS, LANES), F32),
             pltpu.VMEM((2, 2, 5, BS, LANES), F32),
@@ -405,8 +440,8 @@
             pltpu.VMEM((count * (rwidth // LANES), LANES), F32),
             pltpu.VMEM((1920, LANES), F32),
             pltpu.VMEM((20 * BS, LANES), F32),
-            pltpu.VMEM((40 * BS, LANES), F32),
             pltpu.VMEM((10 * BS, LANES), F32),
+            pltpu.VMEM((10, BS, LANES), F32),
             pltpu.VMEM((384, LANES), F32),
             pltpu.VMEM((LANES, LANES), F32),
             pltpu.SemaphoreType.DMA((9,)),
@@ -419,6 +454,15 @@
             collective_id=0, has_side_effects=True, vmem_limit_bytes=62 * 1024 * 1024
         ),
     )(fine2, shell, parent, link)
+    hbm = pl.BlockSpec(memory_space=pltpu.HBM)
+    out, coarse = pl.pallas_call(
+        place,
+        out_shape=(jax.ShapeDtypeStruct(out.shape, F32), jax.ShapeDtypeStruct(coarse.shape, F32)),
+        in_specs=[hbm, hbm],
+        out_specs=(hbm, hbm),
+        scratch_shapes=[pltpu.SemaphoreType.DMA((11,))],
+        compiler_params=pltpu.CompilerParams(vmem_limit_bytes=62 * 1024 * 1024),
+    )(out, coarse)
     return out.reshape(fine.shape), coarse
 
 

time: 30.5 us -> 48.2 us (1.58)
  Pallas kernels: 27 us -> 47.4 us
  local copies, waits for them, and re-layouts: 2.66 us -> 0 us
    pallas_call x0 -> x1, Pallas kernels: none -> 23.5 us  [shards(): pl.pallas_call(place, out_shape=(jax.ShapeDtypeStruct(out.shape, F32), ja...]
    pallas_call x1, Pallas kernels: 27 us -> 23.8 us  [shards(): pl.pallas_call(functools.partial(kernel, n), out_shape=(jax.ShapeDtypeStr...]
    unnamed x4 -> x0, local copies, waits for them, and re-layouts: 2.66 us -> none
where the time goes in v2:
time: 48.2 us; the launch traced here: 48 us
  Pallas kernels  47.4 us (98%)
  between operations  0.64 us (1%)
    pallas_call x1, Pallas kernels, shards(): pl.pallas_call(functools.partial(kernel, n), out_shape=(jax.ShapeDtypeStr...  23.8 us
    pallas_call x1, Pallas kernels, shards(): pl.pallas_call(place, out_shape=(jax.ShapeDtypeStruct(out.shape, F32), ja...  23.5 us

profile of v2, /device:TPU:0, one launch (start us, length us, event | category | flops | bytes accessed | tf_op | source)
XLA Modules:
  0.0 48.0 jit_solution(5484820116585066135)
XLA Ops:
  0.6 23.8 %shard_map.59 = (f32[5,256,128]{2,1,0:T(8,128)}, f32[1,8,2560]{2,1,0:T(8,128)}) custom-call(f32[5,256,128]{2,1,0:T(8,128)} %bitcast.2, f32[1,8,3840]{2,1,0:T(8,128)} %shell_hbm.1, s32[1,64]{1,0:T(1,128)} %parent_hbm.1, s32[6,1,1,8]{3,2,1,0:T(1,128)} %link_hbm.1), custom_call_target="tpu_custom_call" | custom-call | tf_op jit(solution)/shard_map/pallas_call | solution.py:417
  24.5 23.5 %shard_map.60 = (f32[5,256,128]{2,1,0:T(8,128)}, f32[1,8,2560]{2,1,0:T(8,128)}) custom-call(f32[5,256,128]{2,1,0:T(8,128)} %get-tuple-element.6.out, f32[1,8,2560]{2,1,0:T(8,128)} %get-tuple-element.7.coarse), custom_call_target="tpu_custom_call" | custom-call | tf_op jit(solution)/shard_map/pallas_call | solution.py:458

commit v3 on v2

--- a/solution.py
+++ b/solution.py
@@ -62,15 +62,17 @@
     return f, jnp.abs(vd) + sound
 
 
-def interface(ul, fl, sl, ur, fr, sr, sign=0.5):
-    wave = sign * jnp.maximum(sl, sr)
-    return [0.5 * (fl[i] + fr[i]) - wave * (ur[i] - ul[i]) for i in range(5)]
+def interface(ul, fl, sl, ur, fr, sr, sign=None):
+    wave = jnp.maximum(sl, sr)
+    if sign is not None:
+        wave = sign * wave
+    return [(fl[i] + fr[i]) - wave * (ur[i] - ul[i]) for i in range(5)]
 
 
 def kernel(
     n,
     fine, shell_hbm, parent_hbm, link_hbm, out_hbm, coarse,
-    out, shell, parent, link, s0, s1, ypack, zpack, hx, hy, hz, sstage, srecv, rstage, rrecv, xt, cxy, cz, cells_z, xy, zt,
+    out, shell, parent, link, s0, s1, ypack, zpack, hx, hy, hz, sstage, srecv, rstage, rrecv, rstage2, rrecv2, xt, cxy, cz, cells_z, xy, zt,
     load_sem, halo_send, halo_recv, all_send, all_recv,
 ):
     nx, ny, nz = n
@@ -275,7 +277,7 @@
                     total[f] = total[f] + (pltpu.roll(lo, lo.shape[axis] - 1, axis) - lo)
             at = pl.multiple_of(x * BS, BS)
             for f in range(5):
-                dst[f, pl.ds(at, BS), :] = u[f] - LAMBDA * total[f]
+                dst[f, pl.ds(at, BS), :] = u[f] - (0.5 * LAMBDA) * total[f]
             return hxr, un, prn
 
         u = [plane(ref, f, 0) for f in range(5)]
@@ -304,16 +306,16 @@
                     for f in range(5)
                 ]
                 cells = [ref[f, rows, :] for f in range(5)]
-                face = faces(ghost, cells, d, 0.5 - side)
+                face = faces(ghost, cells, d, 1.0 - 2 * side)
                 for f in range(5):
-                    dst[f, rows, :] = dst[f, rows, :] + (LAMBDA - 2 * side * LAMBDA) * face[f]
+                    dst[f, rows, :] = dst[f, rows, :] + (0.5 - side) * LAMBDA * face[f]
         comb = []
         for k in range(2):
             left = pltpu.roll(hz[step, 0, k], 1, 1)
             right = pltpu.roll(hz[step, 1, k], LANES - 1, 1)
             comb.append(jnp.where(even, left, right))
-        sign = jnp.where(even, 0.5, -0.5)
-        scale = jnp.where(even, LAMBDA, -LAMBDA)
+        sign = jnp.where(even, 1.0, -1.0)
+        scale = (0.5 * LAMBDA) * sign
         for g in range(2):
             cells, ghost = [], []
             for f in range(5):
@@ -366,6 +368,7 @@
     interleave = (iota((LANES, 8 * LANES), 0) == iota((LANES, 8 * LANES), 1) // 8).astype(F32).astype(BF16)
     lane8 = iota((blk, LANES), 1) % 8
     sel = beside(sel_tk, blk)
+    back = []
     for c in range((used + LANES - 1) // LANES):
         size = min(LANES, used - c * LANES)
         block = xy[pl.ds(c * LANES, LANES), :]
@@ -378,33 +381,42 @@
         )
         wide = dot(jnp.concatenate(parts_of(rows, 3), axis=0).astype(BF16), interleave, ((1,), (0,)))
         wide = wide[:64] + wide[64:128] + wide[128:]
+        tiles = []
         for g in range(size // 16):
             tile = wide[0:8, g * LANES:(g + 1) * LANES]
             for z in range(1, 8):
                 tile = jnp.where(lane8 == z, wide[z * 8:z * 8 + 8, g * LANES:(g + 1) * LANES], tile)
-            rstage[pl.ds(c * 8 + g, count, stride=rchunks), :] = dot(sel, stacked(tile), ((1,), (0,)))
-    back = exchange(2, rstage, rrecv, 2 * rchunks)
-    for copy in back:
-        copy.wait_recv()
+            tiles.append(tile)
+        routed = dot(sel, stacked(jnp.concatenate(tiles, axis=1)), ((1,), (0,)))
+        stage, first, each = (rstage, 0, 8) if c == 0 else (rstage2, (c - 1) * 8, rchunks - 8)
+        for g in range(size // 16):
+            stage[pl.ds(first + g, count, stride=each), :] = routed[:, g * LANES:(g + 1) * LANES]
+        if c == 0:
+            back.append(exchange(2, rstage, rrecv, 2 * 8))
+    back.append(exchange(3, rstage2, rrecv2, 2 * (rchunks - 8)))
     sel = beside(sel_st, count)
-    for c in range(rchunks):
-        rows = rrecv[pl.ds(c, count, stride=rchunks), :]
-        coarse[0, :, pl.ds(c * LANES, LANES)] = dot(sel, stacked(rows), ((1,), (0,)))
-    for copy in now_copies + mid_copies + back:
+    for half, (recv, first, each) in enumerate(((rrecv, 0, 8), (rrecv2, 8, rchunks - 8))):
+        for copy in back[half]:
+            copy.wait_recv()
+        for c in range(each):
+            rows = recv[pl.ds(c, count, stride=each), :]
+            coarse[0, :, pl.ds((first + c) * LANES, LANES)] = dot(sel, stacked(rows), ((1,), (0,)))
+    for copy in now_copies + mid_copies + back[0] + back[1]:
         copy.wait_send()
     result.wait()
 
 
-def place(out, coarse, out_new, coarse_new, sem):
-    copies = [pltpu.make_async_copy(coarse, coarse_new, sem.at[10])]
-    half = out.shape[1] // 2
-    for f in range(5):
-        for k in range(2):
-            rows = pl.ds(k * half, half)
-            copies.append(pltpu.make_async_copy(out.at[f, rows], out_new.at[f, rows], sem.at[f * 2 + k]))
-    for copy in copies:
+def place(out, coarse, out_new, coarse_new, held, held_coarse, sem):
+    steps = [(coarse, held_coarse, coarse_new)]
+    steps += [(out.at[f], held.at[f], out_new.at[f]) for f in range(5)]
+    loads = [pltpu.make_async_copy(src, mid, sem.at[0, k]) for k, (src, mid, _) in enumerate(steps)]
+    stores = [pltpu.make_async_copy(mid, dst, sem.at[1, k]) for k, (_, mid, dst) in enumerate(steps)]
+    for copy in loads:
         copy.start()
-    for copy in copies:
+    for load, copy in zip(loads, stores):
+        load.wait()
+        copy.start()
+    for copy in stores:
         copy.wait()
 
 
@@ -436,8 +448,10 @@
             pltpu.VMEM((2, 2, 2, BS, LANES), F32),
             pltpu.VMEM((2, count * 16, LANES), F32),
             pltpu.VMEM((2, count * 16, LANES), F32),
-            pltpu.VMEM((count * (rwidth // LANES), LANES), F32),
-            pltpu.VMEM((count * (rwidth // LANES), LANES), F32),
+            pltpu.VMEM((count * 8, LANES), F32),
+            pltpu.VMEM((count * 8, LANES), F32),
+            pltpu.VMEM((count * (rwidth // LANES - 8), LANES), F32),
+            pltpu.VMEM((count * (rwidth // LANES - 8), LANES), F32),
             pltpu.VMEM((1920, LANES), F32),
             pltpu.VMEM((20 * BS, LANES), F32),
             pltpu.VMEM((10 * BS, LANES), F32),
@@ -447,8 +461,8 @@
             pltpu.SemaphoreType.DMA((9,)),
             pltpu.SemaphoreType.DMA((2, 6)),
             pltpu.SemaphoreType.DMA((2, 6)),
-            pltpu.SemaphoreType.DMA((3, group)),
-            pltpu.SemaphoreType.DMA((3, group)),
+            pltpu.SemaphoreType.DMA((4, group)),
+            pltpu.SemaphoreType.DMA((4, group)),
         ],
         compiler_params=pltpu.CompilerParams(
             collective_id=0, has_side_effects=True, vmem_limit_bytes=62 * 1024 * 1024
@@ -460,7 +474,11 @@
         out_shape=(jax.ShapeDtypeStruct(out.shape, F32), jax.ShapeDtypeStruct(coarse.shape, F32)),
         in_specs=[hbm, hbm],
         out_specs=(hbm, hbm),
-        scratch_shapes=[pltpu.SemaphoreType.DMA((11,))],
+        scratch_shapes=[
+            pltpu.VMEM(out.shape, F32),
+            pltpu.VMEM(coarse.shape, F32),
+            pltpu.SemaphoreType.DMA((2, 6)),
+        ],
         compiler_params=pltpu.CompilerParams(vmem_limit_bytes=62 * 1024 * 1024),
     )(out, coarse)
     return out.reshape(fine.shape), coarse

time: 48.2 us -> 26.4 us (0.55)
  Pallas kernels: 47.4 us -> 25.6 us
    pallas_call x1, Pallas kernels: 23.5 us -> 1.96 us  [shards(): pl.pallas_call(place, out_shape=(jax.ShapeDtypeStruct(out.shape, F32), ja...]
where the time goes in v3:
time: 26.4 us; the launch traced here: 26.2 us
  Pallas kernels  25.6 us (97%)
  between operations  0.64 us (2%)
    pallas_call x1, Pallas kernels, shards(): pl.pallas_call(functools.partial(kernel, n), out_shape=(jax.ShapeDtypeStr...  23.6 us
    pallas_call x1, Pallas kernels, shards(): pl.pallas_call(place, out_shape=(jax.ShapeDtypeStruct(out.shape, F32), ja...  1.96 us

profile of v3, /device:TPU:0, one launch (start us, length us, event | category | flops | bytes accessed | tf_op | source)
XLA Modules:
  0.0 26.2 jit_solution(497155893288175367)
XLA Ops:
  0.6 23.6 %shard_map.59 = (f32[5,256,128]{2,1,0:T(8,128)}, f32[1,8,2560]{2,1,0:T(8,128)}) custom-call(f32[5,256,128]{2,1,0:T(8,128)} %bitcast.2, f32[1,8,3840]{2,1,0:T(8,128)} %shell_hbm.1, s32[1,64]{1,0:T(1,128)} %parent_hbm.1, s32[6,1,1,8]{3,2,1,0:T(1,128)} %link_hbm.1), custom_call_target="tpu_custom_call" | custom-call | tf_op jit(solution)/shard_map/pallas_call | solution.py:429
  24.3 2.0 %shard_map.60 = (f32[5,256,128]{2,1,0:T(8,128)}, f32[1,8,2560]{2,1,0:T(8,128)}) custom-call(f32[5,256,128]{2,1,0:T(8,128)} %get-tuple-element.6.out, f32[1,8,2560]{2,1,0:T(8,128)} %get-tuple-element.7.coarse), custom_call_target="tpu_custom_call" | custom-call | tf_op jit(solution)/shard_map/pallas_call | solution.py:472

commit v4 on v3

--- a/solution.py
+++ b/solution.py
@@ -71,8 +71,8 @@
 
 def kernel(
     n,
-    fine, shell_hbm, parent_hbm, link_hbm, out_hbm, coarse,
-    out, shell, parent, link, s0, s1, ypack, zpack, hx, hy, hz, sstage, srecv, rstage, rrecv, rstage2, rrecv2, xt, cxy, cz, cells_z, xy, zt,
+    fine, shell_hbm, parent_hbm, link_hbm, out, coarse,
+    shell, parent, link, s0, s1, ypack, zpack, hx, hy, hz, sstage, srecv, rstage, rrecv, rstage2, rrecv2, xt, cxy, cz, cells_z, xy, zt,
     load_sem, halo_send, halo_recv, all_send, all_recv,
 ):
     nx, ny, nz = n
@@ -139,13 +139,15 @@
 
     loads[1].wait()
     sel = beside(sel_ts, blk)
-    for c in range(chunks):
-        now = shell[0, :, pl.ds(c * LANES, LANES)]
-        end = shell[0, :, pl.ds(width + c * LANES, LANES)]
-        both = jnp.concatenate([stacked(now), stacked(0.5 * (now + end))], axis=1)
-        rows = dot(sel, both, ((1,), (0,)))
-        sstage[0, pl.ds(c, count, stride=16), :] = rows[:, :LANES]
-        sstage[1, pl.ds(c, count, stride=16), :] = rows[:, LANES:]
+
+    def stage_level(level):
+        for c in range(chunks):
+            value = shell[0, :, pl.ds(c * LANES, LANES)]
+            if level:
+                value = 0.5 * (value + shell[0, :, pl.ds(width + c * LANES, LANES)])
+            sstage[level, pl.ds(c, count, stride=16), :] = dot(sel, stacked(value), ((1,), (0,)))
+
+    stage_level(0)
 
     lane = iota((BS, LANES), 1)
     sub = iota((BS, LANES), 0)
@@ -216,7 +218,6 @@
     pack_y(s0)
     pack_z(s0)
     halo0 = halos(s0, 0)
-    mid_copies = exchange(1, sstage.at[1], srecv.at[1], 32)
 
     linkf = jnp.concatenate([link[k, 0] for k in range(6)] + [jnp.zeros((2, blk), jnp.int32)], axis=0)
     over = (iota((blk, LANES), 0) == iota((blk, LANES), 1) // BS).astype(F32).astype(BF16)
@@ -337,6 +338,8 @@
                     dst[f, rows, :] = dst[f, rows, :] + jnp.where(at_end, moved, 0.0)
 
     inner(s0, s1)
+    stage_level(1)
+    mid_copies = exchange(1, sstage.at[1], srecv.at[1], 32)
     for copy in now_copies:
         copy.wait_recv()
     expand(0)
@@ -346,15 +349,13 @@
     pack_y(s1)
     pack_z(s1)
     halo1 = halos(s1, 1)
+    inner(s1, out)
     for copy in mid_copies:
         copy.wait_recv()
     expand(1)
-    inner(s1, out)
     for copy in halo1:
         copy.wait()
     outer(s1, out, 1)
-    result = pltpu.make_async_copy(out, out_hbm, load_sem.at[8])
-    result.start()
 
     for f in range(5):
         for a in range(8):
@@ -403,20 +404,14 @@
             coarse[0, :, pl.ds((first + c) * LANES, LANES)] = dot(sel, stacked(rows), ((1,), (0,)))
     for copy in now_copies + mid_copies + back[0] + back[1]:
         copy.wait_send()
-    result.wait()
-
-
-def place(out, coarse, out_new, coarse_new, held, held_coarse, sem):
-    steps = [(coarse, held_coarse, coarse_new)]
-    steps += [(out.at[f], held.at[f], out_new.at[f]) for f in range(5)]
-    loads = [pltpu.make_async_copy(src, mid, sem.at[0, k]) for k, (src, mid, _) in enumerate(steps)]
-    stores = [pltpu.make_async_copy(mid, dst, sem.at[1, k]) for k, (_, mid, dst) in enumerate(steps)]
-    for copy in loads:
+
+
+def place(out, coarse, out_new, coarse_new, sem):
+    copies = [pltpu.make_async_copy(out.at[f], out_new.at[f], sem.at[f]) for f in range(5)]
+    copies.append(pltpu.make_async_copy(coarse, coarse_new, sem.at[5]))
+    for copy in copies:
         copy.start()
-    for load, copy in zip(loads, stores):
-        load.wait()
-        copy.start()
-    for copy in stores:
+    for copy in copies:
         copy.wait()
 
 
@@ -429,13 +424,12 @@
     out, coarse = pl.pallas_call(
         functools.partial(kernel, n),
         out_shape=(
-            jax.ShapeDtypeStruct((5, BS * BS, LANES), F32),
-            jax.ShapeDtypeStruct((1, shell.shape[1], rwidth), F32),
+            pltpu.VMEM((5, BS * BS, LANES), F32),
+            pltpu.VMEM((1, shell.shape[1], rwidth), F32),
         ),
         in_specs=[pl.BlockSpec(memory_space=pltpu.HBM)] * 4,
-        out_specs=(pl.BlockSpec(memory_space=pltpu.HBM), vmem),
+        out_specs=(vmem, vmem),
         scratch_shapes=[
-            pltpu.VMEM((5, BS * BS, LANES), F32),
             pltpu.VMEM(shell.shape, F32),
             pltpu.VMEM(parent.shape, jnp.int32),
             pltpu.VMEM(link.shape, jnp.int32),
@@ -458,7 +452,7 @@
             pltpu.VMEM((10, BS, LANES), F32),
             pltpu.VMEM((384, LANES), F32),
             pltpu.VMEM((LANES, LANES), F32),
-            pltpu.SemaphoreType.DMA((9,)),
+            pltpu.SemaphoreType.DMA((8,)),
             pltpu.SemaphoreType.DMA((2, 6)),
             pltpu.SemaphoreType.DMA((2, 6)),
             pltpu.SemaphoreType.DMA((4, group)),
@@ -472,14 +466,10 @@
     out, coarse = pl.pallas_call(
         place,
         out_shape=(jax.ShapeDtypeStruct(out.shape, F32), jax.ShapeDtypeStruct(coarse.shape, F32)),
-        in_specs=[hbm, hbm],
+        in_specs=[vmem, vmem],
         out_specs=(hbm, hbm),
-        scratch_shapes=[
-            pltpu.VMEM(out.shape, F32),
-            pltpu.VMEM(coarse.shape, F32),
-            pltpu.SemaphoreType.DMA((2, 6)),
-        ],
-        compiler_params=pltpu.CompilerParams(vmem_limit_bytes=62 * 1024 * 1024),
+        scratch_shapes=[pltpu.SemaphoreType.DMA((6,))],
+        compiler_params=pltpu.CompilerParams(vmem_limit_bytes=4 * 1024 * 1024),
     )(out, coarse)
     return out.reshape(fine.shape), coarse
 

time: 26.4 us -> 24.7 us (0.936)
  Pallas kernels: 25.6 us -> 23.9 us
    pallas_call x1, Pallas kernels: 1.96 us -> 0.91 us  [shards(): pl.pallas_call(place, out_shape=(jax.ShapeDtypeStruct(out.shape, F32), ja...]
    pallas_call x1, Pallas kernels: 23.6 us -> 22.9 us  [shards(): pl.pallas_call(functools.partial(kernel, n), out_shape=(pltpu.VMEM((5, BS...]
where the time goes in v4:
time: 24.7 us; the launch traced here: 24.5 us
  Pallas kernels  23.9 us (97%)
  between operations  0.64 us (3%)
    pallas_call x1, Pallas kernels, shards(): pl.pallas_call(functools.partial(kernel, n), out_shape=(pltpu.VMEM((5, BS...  22.9 us
    pallas_call x1, Pallas kernels, shards(): pl.pallas_call(place, out_shape=(jax.ShapeDtypeStruct(out.shape, F32), ja...  0.91 us

profile of v4, /device:TPU:0, one launch (start us, length us, event | category | flops | bytes accessed | tf_op | source)
XLA Modules:
  0.0 24.5 jit_solution(7658411689687674833)
XLA Ops:
  0.6 22.9 %shard_map.59 = (f32[5,256,128]{2,1,0:T(8,128)S(1)}, f32[1,8,2560]{2,1,0:T(8,128)S(1)}) custom-call(f32[5,256,128]{2,1,0:T(8,128)} %bitcast.2, f32[1,8,3840]{2,1,0:T(8,128)} %shell_hbm.1, s32[1,64]{1,0:T(1,128)} %parent_hbm.1, s32[6,1,1,8]{3,2,1,0:T(1,128)} %link_hbm.1), custom_call_target="tpu_custom_call" | custom-call | tf_op jit(solution)/shard_map/pallas_call | solution.py:424
  23.6 0.9 %shard_map.60 = (f32[5,256,128]{2,1,0:T(8,128)}, f32[1,8,2560]{2,1,0:T(8,128)}) custom-call(f32[5,256,128]{2,1,0:T(8,128)S(1)} %get-tuple-element.6.out, f32[1,8,2560]{2,1,0:T(8,128)S(1)} %get-tuple-element.7.coarse), custom_call_target="tpu_custom_call" | custom-call | tf_op jit(solution)/shard_map/pallas_call | solution.py:466

commit v5 on v4

--- a/solution.py
+++ b/solution.py
@@ -87,7 +87,8 @@
     rchunks = rwidth // LANES
     nq = parent.shape[1]
     peers = []
-    for i in range(1, group):
+    order = sorted(range(1, group), key=lambda i: i % nz == 0)
+    for i in order:
         peer = lax.rem(me + i, group)
         peers.append((gx, peer // nz, lax.rem(peer, nz)))
     xlo, xhi = (lax.rem(gx + nx - 1, nx), gy, gz), (lax.rem(gx + 1, nx), gy, gz)
@@ -122,6 +123,90 @@
     to_t = (jnp.broadcast_to(at_owner, (count, nq)) == iota((count, nq), 0)).astype(F32).astype(BF16)
     mine = (jnp.broadcast_to(par, (blk, nq)) == me * blk + iota((blk, nq), 0)).astype(F32).astype(BF16)
     sel_ts = dot(to_t, mine, ((1,), (1,)))
+
+    loads[1].wait()
+    sel = beside(sel_ts, blk)
+
+    def stage_level(level):
+        for c in range(chunks):
+            value = shell[0, :, pl.ds(c * LANES, LANES)]
+            if level:
+                value = 0.5 * (value + shell[0, :, pl.ds(width + c * LANES, LANES)])
+            sstage[level, pl.ds(c, count, stride=16), :] = dot(sel, stacked(value), ((1,), (0,)))
+
+    stage_level(0)
+
+    lane = iota((BS, LANES), 1)
+    sub = iota((BS, LANES), 0)
+    even = lane % 2 == 0
+    pair = ((lane + 1) // 2) % 8
+    first_pairs = (lane + 1) % LANES < 16
+
+    def plane(ref, f, x):
+        return ref[f, pl.ds(x * BS, BS), :]
+
+    def pack_y(ref, step):
+        for f in range(5):
+            ypack[step, 0, f] = ref[f, pl.ds(0, BS, stride=BS), :]
+            ypack[step, 1, f] = ref[f, pl.ds(BS - 1, BS, stride=BS), :]
+
+    def pack_z(ref, step):
+        packed = [jnp.zeros((BS, LANES), F32)] * 2
+        for f in range(5):
+            for g in range(2):
+                tile = plane(ref, f, 8 * g)
+                for x in range(1, 8):
+                    tile = jnp.where(pair == x, pltpu.roll(plane(ref, f, 8 * g + x), 2 * x, 1), tile)
+                k = f * 2 + g
+                cells_z[k] = tile
+                moved = tile if k % 8 == 0 else pltpu.roll(tile, 16 * (k % 8), 1)
+                packed[k // 8] = jnp.where(((lane + 1) // 16) % 8 == k % 8, moved, packed[k // 8])
+        zpack[step, 0] = packed[0]
+        zpack[step, 1] = packed[1]
+
+    def halos(ref, step):
+        copies = []
+
+        def send(k, src, dst, dev):
+            copy = pltpu.make_async_remote_copy(
+                src_ref=src, dst_ref=dst, send_sem=halo_send.at[step, k], recv_sem=halo_recv.at[step, k],
+                device_id=dev, device_id_type=MESH,
+            )
+            copy.start()
+            copies.append(copy)
+
+        send(0, ref.at[:, pl.ds(BS * BS - BS, BS)], hx.at[step, 0], xhi)
+        send(1, ref.at[:, pl.ds(0, BS)], hx.at[step, 1], xlo)
+        pack_z(ref, step)
+        send(4, zpack.at[step], hz.at[step, 0], zhi)
+        send(5, zpack.at[step], hz.at[step, 1], zlo)
+        pack_y(ref, step)
+        send(2, ypack.at[step, 1], hy.at[step, 0], yhi)
+        send(3, ypack.at[step, 0], hy.at[step, 1], ylo)
+        return copies
+
+    def exchange(kind, stage, recv, rows):
+        copies = []
+        for i, dev in zip(order, peers):
+            to = lax.rem(me + i, group)
+            copy = pltpu.make_async_remote_copy(
+                src_ref=stage.at[pl.ds(pl.multiple_of(to * rows, 8), rows)],
+                dst_ref=recv.at[pl.ds(pl.multiple_of(me * rows, 8), rows)],
+                send_sem=all_send.at[kind, i], recv_sem=all_recv.at[kind, i],
+                device_id=dev, device_id_type=MESH,
+            )
+            copy.start()
+            copies.append(copy)
+        own = pl.ds(pl.multiple_of(me * rows, 8), rows)
+        recv[own, :] = stage[own, :]
+        return copies
+
+    for load in loads[2:]:
+        load.wait()
+    pl.semaphore_wait(barrier, len(greeted))
+    now_copies = exchange(0, sstage.at[0], srecv.at[0], 32)
+    halo0 = halos(s0, 0)
+
     sel_st = dot(mine, to_t, ((1,), (1,)))
     at_block8 = jnp.broadcast_to(at_block.astype(F32), (8, nq)).astype(BF16)
     spread = (iota((nq, LANES), 0) == me * blk + iota((nq, LANES), 1) // BS).astype(F32).astype(BF16)
@@ -137,87 +222,6 @@
     be3_hi = jnp.concatenate([be_hi] * 3, axis=0).astype(BF16)
     sel_tk = (jnp.broadcast_to(row_blk, (count, blk)) == iota((count, blk), 0).astype(F32)).astype(F32)
 
-    loads[1].wait()
-    sel = beside(sel_ts, blk)
-
-    def stage_level(level):
-        for c in range(chunks):
-            value = shell[0, :, pl.ds(c * LANES, LANES)]
-            if level:
-                value = 0.5 * (value + shell[0, :, pl.ds(width + c * LANES, LANES)])
-            sstage[level, pl.ds(c, count, stride=16), :] = dot(sel, stacked(value), ((1,), (0,)))
-
-    stage_level(0)
-
-    lane = iota((BS, LANES), 1)
-    sub = iota((BS, LANES), 0)
-    even = lane % 2 == 0
-    pair = ((lane + 1) // 2) % 8
-    first_pairs = (lane + 1) % LANES < 16
-
-    def plane(ref, f, x):
-        return ref[f, pl.ds(x * BS, BS), :]
-
-    def pack_y(ref):
-        for f in range(5):
-            ypack[0, f] = ref[f, pl.ds(0, BS, stride=BS), :]
-            ypack[1, f] = ref[f, pl.ds(BS - 1, BS, stride=BS), :]
-
-    def pack_z(ref):
-        packed = [jnp.zeros((BS, LANES), F32)] * 2
-        for f in range(5):
-            for g in range(2):
-                tile = plane(ref, f, 8 * g)
-                for x in range(1, 8):
-                    tile = jnp.where(pair == x, pltpu.roll(plane(ref, f, 8 * g + x), 2 * x, 1), tile)
-                k = f * 2 + g
-                cells_z[k] = tile
-                moved = tile if k % 8 == 0 else pltpu.roll(tile, 16 * (k % 8), 1)
-                packed[k // 8] = jnp.where(((lane + 1) // 16) % 8 == k % 8, moved, packed[k // 8])
-        zpack[0] = packed[0]
-        zpack[1] = packed[1]
-
-    def halos(ref, step):
-        def send(k, src, dst, dev):
-            copy = pltpu.make_async_remote_copy(
-                src_ref=src, dst_ref=dst, send_sem=halo_send.at[step, k], recv_sem=halo_recv.at[step, k],
-                device_id=dev, device_id_type=MESH,
-            )
-            copy.start()
-            return copy
-
-        return [
-            send(0, ref.at[:, pl.ds(BS * BS - BS, BS)], hx.at[step, 0], xhi),
-            send(1, ref.at[:, pl.ds(0, BS)], hx.at[step, 1], xlo),
-            send(2, ypack.at[1], hy.at[step, 0], yhi),
-            send(3, ypack.at[0], hy.at[step, 1], ylo),
-            send(4, zpack, hz.at[step, 0], zhi),
-            send(5, zpack, hz.at[step, 1], zlo),
-        ]
-
-    def exchange(kind, stage, recv, rows):
-        copies = []
-        for i, dev in enumerate(peers):
-            to = lax.rem(me + i + 1, group)
-            copy = pltpu.make_async_remote_copy(
-                src_ref=stage.at[pl.ds(pl.multiple_of(to * rows, 8), rows)],
-                dst_ref=recv.at[pl.ds(pl.multiple_of(me * rows, 8), rows)],
-                send_sem=all_send.at[kind, i], recv_sem=all_recv.at[kind, i],
-                device_id=dev, device_id_type=MESH,
-            )
-            copy.start()
-            copies.append(copy)
-        own = pl.ds(pl.multiple_of(me * rows, 8), rows)
-        recv[own, :] = stage[own, :]
-        return copies
-
-    for load in loads[2:]:
-        load.wait()
-    pl.semaphore_wait(barrier, len(greeted))
-    now_copies = exchange(0, sstage.at[0], srecv.at[0], 32)
-    pack_y(s0)
-    pack_z(s0)
-    halo0 = halos(s0, 0)
 
     linkf = jnp.concatenate([link[k, 0] for k in range(6)] + [jnp.zeros((2, blk), jnp.int32)], axis=0)
     over = (iota((blk, LANES), 0) == iota((blk, LANES), 1) // BS).astype(F32).astype(BF16)
@@ -293,7 +297,7 @@
         cf, cs = flux(cells, prim(cells), d)
         return interface(ghost, gf, gs, cells, cf, cs, sign)
 
-    def outer(ref, dst, step):
+    def outer(ref, dst, step, after):
         for d in range(2):
             for side in range(2):
                 chosen = jnp.broadcast_to(mask[2 * d + side:2 * d + side + 1], (BS, LANES)) > 0.5
@@ -336,6 +340,7 @@
                     moved = change if x == 0 else pltpu.roll(change, LANES - 2 * x, 1)
                     rows = pl.ds((8 * g + x) * BS, BS)
                     dst[f, rows, :] = dst[f, rows, :] + jnp.where(at_end, moved, 0.0)
+            after(g)
 
     inner(s0, s1)
     stage_level(1)
@@ -345,9 +350,7 @@
     expand(0)
     for copy in halo0:
         copy.wait()
-    outer(s0, s1, 0)
-    pack_y(s1)
-    pack_z(s1)
+    outer(s0, s1, 0, lambda g: None)
     halo1 = halos(s1, 1)
     inner(s1, out)
     for copy in mid_copies:
@@ -355,22 +358,22 @@
     expand(1)
     for copy in halo1:
         copy.wait()
-    outer(s1, out, 1)
-
-    for f in range(5):
-        for a in range(8):
-            total = None
-            for x in range(2):
-                for y in range(2):
-                    piece = out[f, pl.ds((2 * a + x) * BS + y, 8, stride=2), :]
-                    total = piece if total is None else total + piece
-            xy[pl.ds((f * 8 + a) * 8, 8), :] = 0.125 * total
-    used = 5 * 64
     interleave = (iota((LANES, 8 * LANES), 0) == iota((LANES, 8 * LANES), 1) // 8).astype(F32).astype(BF16)
     lane8 = iota((blk, LANES), 1) % 8
-    sel = beside(sel_tk, blk)
-    back = []
-    for c in range((used + LANES - 1) // LANES):
+    used = 5 * 64
+    sel_rows = beside(sel_tk, blk)
+
+    def means(g):
+        for f in range(5):
+            for a in range(4):
+                total = None
+                for x in range(2):
+                    for y in range(2):
+                        piece = out[f, pl.ds((8 * g + 2 * a + x) * BS + y, 8, stride=2), :]
+                        total = piece if total is None else total + piece
+                xy[pl.ds(g * 160 + f * 32 + a * 8, 8), :] = 0.125 * total
+
+    def rows_out(c):
         size = min(LANES, used - c * LANES)
         block = xy[pl.ds(c * LANES, LANES), :]
         if size < LANES:
@@ -388,20 +391,33 @@
             for z in range(1, 8):
                 tile = jnp.where(lane8 == z, wide[z * 8:z * 8 + 8, g * LANES:(g + 1) * LANES], tile)
             tiles.append(tile)
-        routed = dot(sel, stacked(jnp.concatenate(tiles, axis=1)), ((1,), (0,)))
+        routed = dot(sel_rows, stacked(jnp.concatenate(tiles, axis=1)), ((1,), (0,)))
         stage, first, each = (rstage, 0, 8) if c == 0 else (rstage2, (c - 1) * 8, rchunks - 8)
         for g in range(size // 16):
             stage[pl.ds(first + g, count, stride=each), :] = routed[:, g * LANES:(g + 1) * LANES]
-        if c == 0:
+
+    back = []
+
+    def after(g):
+        means(g)
+        if g == 0:
+            rows_out(0)
             back.append(exchange(2, rstage, rrecv, 2 * 8))
-    back.append(exchange(3, rstage2, rrecv2, 2 * (rchunks - 8)))
+        else:
+            rows_out(1)
+            rows_out(2)
+            back.append(exchange(3, rstage2, rrecv2, 2 * (rchunks - 8)))
+
+    outer(s1, out, 1, after)
     sel = beside(sel_st, count)
     for half, (recv, first, each) in enumerate(((rrecv, 0, 8), (rrecv2, 8, rchunks - 8))):
         for copy in back[half]:
             copy.wait_recv()
         for c in range(each):
             rows = recv[pl.ds(c, count, stride=each), :]
-            coarse[0, :, pl.ds((first + c) * LANES, LANES)] = dot(sel, stacked(rows), ((1,), (0,)))
+            start = (first + c) * 16
+            g, f, pairs = start // 160, start % 160 // 32, start % 32 // 16
+            coarse[0, :, pl.ds((f * 4 + 2 * g + pairs) * LANES, LANES)] = dot(sel, stacked(rows), ((1,), (0,)))
     for copy in now_copies + mid_copies + back[0] + back[1]:
         copy.wait_send()
 
@@ -435,8 +451,8 @@
             pltpu.VMEM(link.shape, jnp.int32),
             pltpu.VMEM((5, BS * BS, LANES), F32),
             pltpu.VMEM((5, BS * BS, LANES), F32),
-            pltpu.VMEM((2, 5, BS, LANES), F32),
-            pltpu.VMEM((2, BS, LANES), F32),
+            pltpu.VMEM((2, 2, 5, BS, LANES), F32),
+            pltpu.VMEM((2, 2, BS, LANES), F32),
             pltpu.VMEM((2, 2, 5, BS, LANES), F32),
             pltpu.VMEM((2, 2, 5, BS, LANES), F32),
             pltpu.VMEM((2, 2, 2, BS, LANES), F32),

time: 24.7 us -> 24.7 us (level)
  no operation moved by 1% of the time
where the time goes in v5:
time: 24.7 us; the launch traced here: 24.6 us
  Pallas kernels  23.9 us (97%)
  between operations  0.64 us (3%)
    pallas_call x1, Pallas kernels, shards(): pl.pallas_call(functools.partial(kernel, n), out_shape=(pltpu.VMEM((5, BS...  23 us
    pallas_call x1, Pallas kernels, shards(): pl.pallas_call(place, out_shape=(jax.ShapeDtypeStruct(out.shape, F32), ja...  0.91 us

profile of v5, /device:TPU:0, one launch (start us, length us, event | category | flops | bytes accessed | tf_op | source)
XLA Modules:
  0.0 24.6 jit_solution(2077102315689242196)
XLA Ops:
  0.6 23.0 %shard_map.59 = (f32[5,256,128]{2,1,0:T(8,128)S(1)}, f32[1,8,2560]{2,1,0:T(8,128)S(1)}) custom-call(f32[5,256,128]{2,1,0:T(8,128)} %bitcast.2, f32[1,8,3840]{2,1,0:T(8,128)} %shell_hbm.1, s32[1,64]{1,0:T(1,128)} %parent_hbm.1, s32[6,1,1,8]{3,2,1,0:T(1,128)} %link_hbm.1), custom_call_target="tpu_custom_call" | custom-call | tf_op jit(solution)/shard_map/pallas_call | solution.py:440
  23.7 0.9 %shard_map.60 = (f32[5,256,128]{2,1,0:T(8,128)}, f32[1,8,2560]{2,1,0:T(8,128)}) custom-call(f32[5,256,128]{2,1,0:T(8,128)S(1)} %get-tuple-element.6.out, f32[1,8,2560]{2,1,0:T(8,128)S(1)} %get-tuple-element.7.coarse), custom_call_target="tpu_custom_call" | custom-call | tf_op jit(solution)/shard_map/pallas_call | solution.py:482

commit v6 on v5

--- a/solution.py
+++ b/solution.py
@@ -259,38 +259,57 @@
             cz[pl.ds(k * BS, 8, stride=2), :] = tile
             cz[pl.ds(k * BS + 1, 8, stride=2), :] = tile
 
+    def across(u, pr, d, edge):
+        axis = d - 1
+        fc, sc = flux(u, pr, d)
+        ub = [pltpu.roll(a, 1, axis) for a in u]
+        fb = [ub[1 + d] if i == 0 else pltpu.roll(fc[i], 1, axis) for i in range(5)]
+        low = interface(ub, fb, pltpu.roll(sc, 1, axis), u, fc, sc)
+        low = [jnp.where(edge, 0.0, a) for a in low]
+        return [pltpu.roll(a, a.shape[axis] - 1, axis) - a for a in low]
+
+    is_lo8 = iota((8, LANES), 1) % BS == 0
+
     def inner(ref, dst):
-        def step_x(x, hxl, u, pr, last):
-            if last:
-                total = [-hxl[f] for f in range(5)]
-                hxr, un, prn = hxl, u, pr
-            else:
-                at = pl.multiple_of((x + 1) * BS, BS)
-                un = [ref[f, pl.ds(at, BS), :] for f in range(5)]
-                prn = prim(un)
-                fc, sc = flux(u, pr, 0)
-                fn, sn = flux(un, prn, 0)
-                hxr = interface(u, fc, sc, un, fn, sn)
-                total = [hxr[f] - hxl[f] for f in range(5)]
-            for d, axis, edge in ((1, 0, sub == 0), (2, 1, is_lo)):
-                fc, sc = flux(u, pr, d)
-                ub = [pltpu.roll(a, 1, axis) for a in u]
-                fb = [pltpu.roll(a, 1, axis) for a in fc]
-                low = interface(ub, fb, pltpu.roll(sc, 1, axis), u, fc, sc)
+        def along_xz(half):
+            def tile(f, x):
+                return ref[f, pl.ds(pl.multiple_of(x * BS + half, 8), 8), :]
+
+            def step_x(x, hxl, u, pr, last):
+                if last:
+                    total = [-a for a in hxl]
+                    hxr, un, prn = hxl, u, pr
+                else:
+                    un = [tile(f, x + 1) for f in range(5)]
+                    prn = prim(un)
+                    fc, sc = flux(u, pr, 0)
+                    fn, sn = flux(un, prn, 0)
+                    hxr = interface(u, fc, sc, un, fn, sn)
+                    total = [hxr[f] - hxl[f] for f in range(5)]
+                change = across(u, pr, 2, is_lo8)
+                at = pl.multiple_of(x * BS + half, 8)
                 for f in range(5):
-                    lo = jnp.where(edge, 0.0, low[f])
-                    total[f] = total[f] + (pltpu.roll(lo, lo.shape[axis] - 1, axis) - lo)
-            at = pl.multiple_of(x * BS, BS)
+                    dst[f, pl.ds(at, 8), :] = u[f] - (0.5 * LAMBDA) * (total[f] + change[f])
+                return hxr, un, prn
+
+            u = [tile(f, 0) for f in range(5)]
+            zero = [jnp.zeros((8, LANES), F32)] * 5
+            carry = lax.fori_loop(
+                0, BS - 1, lambda x, carry: step_x(x, *carry, False), (zero, u, prim(u)), unroll=3
+            )
+            step_x(BS - 1, *carry, True)
+
+        def along_y(x, carry):
+            at = pl.ds(pl.multiple_of(x * BS, BS), BS)
+            u = [ref[f, at, :] for f in range(5)]
+            change = across(u, prim(u), 1, sub == 0)
             for f in range(5):
-                dst[f, pl.ds(at, BS), :] = u[f] - (0.5 * LAMBDA) * total[f]
-            return hxr, un, prn
-
-        u = [plane(ref, f, 0) for f in range(5)]
-        zero = [jnp.zeros((BS, LANES), F32)] * 5
-        carry = lax.fori_loop(
-            0, BS - 1, lambda x, carry: step_x(x, *carry, False), (zero, u, prim(u)), unroll=3
-        )
-        step_x(BS - 1, *carry, True)
+                dst[f, at, :] = dst[f, at, :] - (0.5 * LAMBDA) * change[f]
+            return carry
+
+        along_xz(0)
+        along_xz(8)
+        lax.fori_loop(0, BS, along_y, 0, unroll=2)
 
     def faces(ghost, cells, d, sign):
         gf, gs = flux(ghost, prim(ghost), d)

time: 24.7 us -> 24.2 us (0.980)
  Pallas kernels: 23.9 us -> 23.4 us
    pallas_call x1, Pallas kernels: 23 us -> 22.5 us  [shards(): pl.pallas_call(functools.partial(kernel, n), out_shape=(pltpu.VMEM((5, BS...]
where the time goes in v6:
time: 24.2 us; the launch traced here: 24.1 us
  Pallas kernels  23.4 us (97%)
  between operations  0.64 us (3%)
    pallas_call x1, Pallas kernels, shards(): pl.pallas_call(functools.partial(kernel, n), out_shape=(pltpu.VMEM((5, BS...  22.5 us
    pallas_call x1, Pallas kernels, shards(): pl.pallas_call(place, out_shape=(jax.ShapeDtypeStruct(out.shape, F32), ja...  0.91 us

profile of v6, /device:TPU:0, one launch (start us, length us, event | category | flops | bytes accessed | tf_op | source)
XLA Modules:
  0.0 24.1 jit_solution(17666590226170945109)
XLA Ops:
  0.6 22.5 %shard_map.59 = (f32[5,256,128]{2,1,0:T(8,128)S(1)}, f32[1,8,2560]{2,1,0:T(8,128)S(1)}) custom-call(f32[5,256,128]{2,1,0:T(8,128)} %bitcast.2, f32[1,8,3840]{2,1,0:T(8,128)} %shell_hbm.1, s32[1,64]{1,0:T(1,128)} %parent_hbm.1, s32[6,1,1,8]{3,2,1,0:T(1,128)} %link_hbm.1), custom_call_target="tpu_custom_call" | custom-call | tf_op jit(solution)/shard_map/pallas_call | solution.py:459
  23.2 0.9 %shard_map.60 = (f32[5,256,128]{2,1,0:T(8,128)}, f32[1,8,2560]{2,1,0:T(8,128)}) custom-call(f32[5,256,128]{2,1,0:T(8,128)S(1)} %get-tuple-element.6.out, f32[1,8,2560]{2,1,0:T(8,128)S(1)} %get-tuple-element.7.coarse), custom_call_target="tpu_custom_call" | custom-call | tf_op jit(solution)/shard_map/pallas_call | solution.py:501

commit v7 on v6

--- a/solution.py
+++ b/solution.py
@@ -295,7 +295,7 @@
             u = [tile(f, 0) for f in range(5)]
             zero = [jnp.zeros((8, LANES), F32)] * 5
             carry = lax.fori_loop(
-                0, BS - 1, lambda x, carry: step_x(x, *carry, False), (zero, u, prim(u)), unroll=3
+                0, BS - 1, lambda x, carry: step_x(x, *carry, False), (zero, u, prim(u)), unroll=5
             )
             step_x(BS - 1, *carry, True)
 
@@ -309,7 +309,7 @@
 
         along_xz(0)
         along_xz(8)
-        lax.fori_loop(0, BS, along_y, 0, unroll=2)
+        lax.fori_loop(0, BS, along_y, 0, unroll=4)
 
     def faces(ghost, cells, d, sign):
         gf, gs = flux(ghost, prim(ghost), d)

time: 24.2 us -> 24.3 us (level)
  no operation moved by 1% of the time
where the time goes in v7:
time: 24.3 us; the launch traced here: 24.2 us
  Pallas kernels  23.5 us (97%)
  between operations  0.64 us (3%)
    pallas_call x1, Pallas kernels, shards(): pl.pallas_call(functools.partial(kernel, n), out_shape=(pltpu.VMEM((5, BS...  22.6 us
    pallas_call x1, Pallas kernels, shards(): pl.pallas_call(place, out_shape=(jax.ShapeDtypeStruct(out.shape, F32), ja...  0.91 us

profile of v7, /device:TPU:0, one launch (start us, length us, event | category | flops | bytes accessed | tf_op | source)
XLA Modules:
  0.0 24.2 jit_solution(3179498596562932647)
XLA Ops:
  0.6 22.6 %shard_map.59 = (f32[5,256,128]{2,1,0:T(8,128)S(1)}, f32[1,8,2560]{2,1,0:T(8,128)S(1)}) custom-call(f32[5,256,128]{2,1,0:T(8,128)} %bitcast.2, f32[1,8,3840]{2,1,0:T(8,128)} %shell_hbm.1, s32[1,64]{1,0:T(1,128)} %parent_hbm.1, s32[6,1,1,8]{3,2,1,0:T(1,128)} %link_hbm.1), custom_call_target="tpu_custom_call" | custom-call | tf_op jit(solution)/shard_map/pallas_call | solution.py:459
  23.3 0.9 %shard_map.60 = (f32[5,256,128]{2,1,0:T(8,128)}, f32[1,8,2560]{2,1,0:T(8,128)}) custom-call(f32[5,256,128]{2,1,0:T(8,128)S(1)} %get-tuple-element.6.out, f32[1,8,2560]{2,1,0:T(8,128)S(1)} %get-tuple-element.7.coarse), custom_call_target="tpu_custom_call" | custom-call | tf_op jit(solution)/shard_map/pallas_call | solution.py:501
